TPU v7x, 768 devices: a whole 4x8x12 slice. The times are simulated.
768 devices in a mesh: replica: 96 (over y_hi, z, core), fsdp: 8 (over x, y_lo).
Axes of the slice: x: 4, y: 8 (y_hi: 4, y_lo: 2; y = y_hi * 2 + y_lo), z: 12, core: 2. Of those that a mesh axis runs over, the one named last changes fastest.
Arguments:
- pseudo_grad: bfloat16 [96, 8192, 512], P('replica', 'fsdp'), may hold values from -448 to 448
- block_exponent: int32 [96, 8192, 4], P('replica', 'fsdp'), may hold values from -10 to -6
- base_params: bfloat16 [8192, 512], P('fsdp'), may hold values from -0.29882812 to 0.29882812
- outer_momentum: float32 [8192, 512], P('fsdp'), may hold values from -0.3 to 0.3
- tokens: bfloat16 [98304, 8192], P(('replica', 'fsdp')), may hold values from -6 to 6
- norm_gain: bfloat16 [8192], replicated, may hold values from 0.5 to 1.5
- kv_weight: bfloat16 [2, 8192, 512], P(None, 'fsdp'), may hold values from -0.0625 to 0.0625
Outputs:
- new_params: bfloat16 [8192, 512], P('fsdp')
- new_momentum: float32 [8192, 512], P('fsdp')
- keys_values: bfloat16 [98304, 1024], P(('replica', 'fsdp'))
All inputs are finite; a program needn't handle non-finite values.
Results may differ from a plain program's by a relative error of at most 0.0049.
Values may be sent and summed in bfloat16 or wider, within the bound.
No kernel may reach another device: no remote copies, remote signals or barrier semaphores. Data moves between devices by JAX's collectives and lax.ppermute only.
A program may use at most 128 MiB of HBM per device.

v0:
```python
import jax
import jax.numpy as jnp
from jax import lax
from jax.sharding import PartitionSpec as P

outer_rate = 0.7
momentum_coef = 0.9


def dequantize(values, exponents):
    rows = values.shape[0]
    blocks = exponents.shape[1]
    scale = jnp.exp2(exponents.astype(jnp.float32))
    shaped = values.astype(jnp.float32).reshape(rows, blocks, -1) * scale[:, :, None]
    return shaped.reshape(rows, -1)


def outer_update(pseudo_grad, block_exponent, base_params, outer_momentum):
    delta = dequantize(pseudo_grad[0], block_exponent[0])
    count = lax.axis_size("replica")
    average = lax.psum(delta, "replica") / count
    new_momentum = momentum_coef * outer_momentum + average
    new_params = (
        base_params.astype(jnp.float32) - outer_rate * (average + momentum_coef * new_momentum)
    ).astype(jnp.bfloat16)
    return (new_params, new_momentum)


def inner_project(tokens, norm_gain, kv_weight):
    wide = tokens.astype(jnp.float32)
    meansq = jnp.mean(wide * wide, axis=-1, keepdims=True)
    normed = (wide * lax.rsqrt(meansq + 1e-05) * norm_gain.astype(jnp.float32)).astype(jnp.bfloat16)
    width = kv_weight.shape[2]
    total = jnp.einsum(
        "tn,knh->tkh",
        normed,
        lax.all_gather(kv_weight, "fsdp", axis=1, tiled=True),
        preferred_element_type=jnp.float32,
    )
    return total.reshape(tokens.shape[0], 2 * width).astype(jnp.bfloat16)


def body(pseudo_grad, block_exponent, base_params, outer_momentum, tokens, norm_gain, kv_weight):
    keys_values = inner_project(tokens, norm_gain, kv_weight)
    new_params, new_momentum = outer_update(
        pseudo_grad, block_exponent, base_params, outer_momentum
    )
    return (new_params, new_momentum, keys_values)


def solution(mesh):
    placed = (
        P("replica", "fsdp", None),
        P("replica", "fsdp", None),
        P("fsdp", None),
        P("fsdp", None),
        P(("replica", "fsdp"), None),
        P(),
        P(None, "fsdp", None),
    )
    return jax.shard_map(
        body,
        mesh=mesh,
        in_specs=placed,
        out_specs=(P("fsdp", None), P("fsdp", None), P(("replica", "fsdp"), None)),
        check_vma=False,
    )
```

profile of v0, /device:TPU:1, one launch (start us, length us, event | category | flops | bytes accessed | tf_op | source)
XLA Modules:
  0.0 865.1 jit_solution(15626323479624261037)
XLA Ops:
  8.0 0.0 all-reduce.2.cloned.1.call-start
  8.0 0.7 exponential_bitcast_fusion
  8.8 0.2 copy.11
  9.0 0.0 copy-start.1
  9.0 1.2 mul.42
  10.3 0.0 copy-done.1
  10.3 1.7 bitcast_multiply_fusion
  12.0 0.0 copy-start.3
  12.0 0.0 copy-start
  12.0 0.0 all-reduce.2.cloned.1.call-update
  12.0 0.0 copy-start.2
  12.0 0.0 all-gather.2.cloned.1.call-start
  12.0 0.5 all-gather.2.cloned.1.call-update
  12.6 0.1 copy-done.3
  12.7 0.9 copy-done
  13.6 0.5 fusion
  14.1 829.9 %all-reduce.2.cloned.1.call-done = f32[1024,512]{1,0:T(8,128)} async-done(((f32[1024,512]{1,0:T(8,128)}), f32[1024,512]{1,0:T(8,128)}) %all-reduce.2.cloned.1.call-update) | async-done | bytes 2097168 | tf_op jit(solution)/shard_map/psum | solution.py:21
  844.0 0.0 copy-done.2
  844.0 4.5 subtract_convert_fusion
  848.5 0.0 all-gather.2.cloned.1.call-done
  848.5 8.1 fusion.8
  856.7 0.2 copy.12
  856.8 0.9 copy.13
  (2 shorter events, 0.0 us)
Async XLA Ops:
  8.0 836.0 %all-reduce.2.cloned.1.call-start = ((), (), s32[]{:S(2)}) async-start(), calls=%async_computation | async-start | bytes 4194304 | tf_op jit(solution)/shard_map/psum | solution.py:21
  9.0 1.3 copy-start.1
  12.0 0.7 copy-start.3
  12.0 1.6 copy-start
  12.0 832.0 %copy-start.2 = (bf16[1024,512]{1,0:T(8,128)(2,1)S(1)}, bf16[1024,512]{1,0:T(8,128)(2,1)}, u32[]{:S(2)}) copy-start(bf16[1024,512]{1,0:T(8,128)(2,1)} %param.9) | copy-start | bytes 3145732
  12.0 836.5 %all-gather.2.cloned.1.call-start = ((), (), s32[]{:S(2)}) async-start(), calls=%async_computation.1 | async-start | bytes 18874368 | tf_op jit(solution)/shard_map/all_gather | solution.py:37
Sparse Core Ops, SparseCore 0:
  12.6 831.3 all-reduce.1
Sparse Core Ops, SparseCore 1:
  15.1 357.9 all-gather.1
where the time goes:
time: 868 us; the launch traced here: 865 us
  waiting for transfers between devices  830 us (96%)
  between operations  15.5 us (2%)
    psum x1, waiting for transfers between devices, outer_update(): average = lax.psum(delta, 'replica') / count  830 us
  transfers between devices with their start and end apart: 2, of which 1 were waited for; matrix products, arithmetic and copies ran while one was open for 1% of the time, Pallas kernels for 0%

commit v1 on v0

v1 whole, which is shorter than its diff:
```python
import functools

import jax
import jax.numpy as jnp
from jax import lax
from jax.experimental import pallas as pl
from jax.experimental.pallas import tpu as pltpu
from jax.sharding import Mesh
from jax.sharding import PartitionSpec as P

outer_rate = 0.7
momentum_coef = 0.9
f32, bf16 = jnp.float32, jnp.bfloat16
VMEM_LIMIT = 48 * 1024 * 1024

SHAPE = (4, 3, 4, 2, 4, 2)
NAMES = ("yh", "zh", "zl", "core", "x", "yl")
REPLICA = ("yh", "zh", "zl", "core")
FSDP = ("x", "yl")
GROUP = ("yh", "zl")


def vmem():
    return pl.BlockSpec(memory_space=pltpu.VMEM)


def smem():
    return pl.BlockSpec(memory_space=pltpu.SMEM)


def params():
    return pltpu.CompilerParams(vmem_limit_bytes=VMEM_LIMIT)


def shift(value, axis, by):
    n = lax.axis_size(axis)
    return lax.ppermute(value, axis, [(i, (i + by) % n) for i in range(n)])


def dequantize_kernel(place, values, exponents, keep, send):
    half, width = keep.shape
    blocks = exponents.shape[0]
    core = place[2]
    scale = jnp.exp2(exponents[...].astype(f32))
    lane = lax.broadcasted_iota(jnp.int32, (blocks, width), 1)
    row = lax.broadcasted_iota(jnp.int32, (blocks, width), 0)
    spread = jnp.where(lane // (width // blocks) == row, 1.0, 0.0).astype(f32)
    for out, part in ((keep, core), (send, 1 - core)):
        start = pl.multiple_of(part * half, half)
        mine = jnp.where(part == 0, scale[:, :half], scale[:, half:])
        wide = lax.dot_general(
            mine.astype(bf16),
            spread.astype(bf16),
            (((0,), (0,)), ((), ())),
            preferred_element_type=f32,
        )
        out[...] = (values[pl.ds(start, half), :].astype(f32) * wide).astype(bf16)


def dequantize(place, values, exponents):
    rows, width = values.shape
    half = jax.ShapeDtypeStruct((rows // 2, width), bf16)
    return pl.pallas_call(
        dequantize_kernel,
        out_shape=(half, half),
        in_specs=[smem(), vmem(), vmem()],
        out_specs=(vmem(), vmem()),
        compiler_params=params(),
        cost_estimate=pl.CostEstimate(
            flops=4 * rows * width, bytes_accessed=4 * rows * width, transcendentals=0
        ),
        name="dequantize",
    )(place, values, exponents)


def update_kernel(place, own, other, base, momentum, new_params, new_momentum):
    step = pl.program_id(0)
    steps = pl.num_programs(0)

    def run(average):
        average = average.astype(f32)
        fresh = momentum_coef * momentum[...] + average
        new_momentum[...] = fresh
        new_params[...] = (
            base[...].astype(f32) - outer_rate * (average + momentum_coef * fresh)
        ).astype(bf16)

    @pl.when(step < steps // 2)
    def _():
        run(own[...])

    @pl.when(step >= steps // 2)
    def _():
        run(other[...])


def update(place, own, other, base, momentum):
    rows, width = base.shape
    steps = 4
    each = rows // steps
    near = steps // 2

    def row(i, place):
        return (lax.rem(i + place[2] * near, steps), 0)

    return pl.pallas_call(
        update_kernel,
        out_shape=(
            jax.ShapeDtypeStruct((rows, width), bf16),
            jax.ShapeDtypeStruct((rows, width), f32),
        ),
        grid_spec=pltpu.PrefetchScalarGridSpec(
            num_scalar_prefetch=1,
            grid=(steps,),
            in_specs=[
                pl.BlockSpec((each, width), lambda i, place: (jnp.minimum(i, near - 1), 0)),
                pl.BlockSpec((each, width), lambda i, place: (jnp.maximum(i - near, 0), 0)),
                pl.BlockSpec((each, width), row),
                pl.BlockSpec((each, width), row),
            ],
            out_specs=[pl.BlockSpec((each, width), row), pl.BlockSpec((each, width), row)],
        ),
        compiler_params=params(),
        cost_estimate=pl.CostEstimate(
            flops=8 * rows * width, bytes_accessed=14 * rows * width, transcendentals=0
        ),
        name="update",
    )(place, own, other, base, momentum)


def gather_group(value):
    group = lax.axis_size(GROUP)
    value = lax.all_to_all(
        jnp.broadcast_to(value, (group, *value.shape)), GROUP, 0, 0, tiled=True
    )
    return value.reshape(-1, value.shape[-1])


def scatter_group(value):
    group = lax.axis_size(GROUP)
    parts = value.reshape(group, value.shape[0] // group, value.shape[1])
    parts = lax.all_to_all(parts, GROUP, 0, 0, tiled=True)
    return jnp.sum(parts.astype(f32), axis=0)


def sum_thirds(value):
    third = lax.axis_size("zh")
    whole = lax.all_to_all(
        jnp.broadcast_to(value, (third, *value.shape)), "zh", 0, 0, tiled=True
    )
    return jnp.sum(whole, axis=0)


def norm_kernel(place, tokens, gain, weight, *refs):
    outs, share, done = refs[:-2], refs[-2], refs[-1]
    x, yl, core = place[0], place[1], place[2]
    rows = share.shape[1]
    copy = pltpu.make_async_copy(
        weight.at[:, pl.ds(pl.multiple_of(core * rows, rows), rows), :], share, done
    )
    copy.start()
    peers = len(outs)
    width = tokens.shape[1]
    block = width // peers
    half, quarter = block // 2, block // 4
    total = jnp.zeros((tokens.shape[0], 128), f32)
    for at in range(0, width, 128):
        piece = tokens[:, at : at + 128].astype(f32)
        total += piece * piece
    meansq = jnp.sum(total, axis=1, keepdims=True) / width
    scale = lax.rsqrt(meansq + 1e-05)
    for k, out in enumerate(outs):
        first = lax.rem(x + k, peers) * block
        for at, start, size in (
            (0, yl * half, half),
            (half, (1 - yl) * half + core * quarter, quarter),
            (half + quarter, (1 - yl) * half + (1 - core) * quarter, quarter),
        ):
            columns = pl.ds(pl.multiple_of(first + start, quarter), size)
            piece = tokens[:, columns].astype(f32) * scale * gain[:, columns].astype(f32)
            out[:, at : at + size] = piece.astype(bf16)
    copy.wait()


def normalize(place, tokens, gain, weight):
    rows, width = tokens.shape
    peers = lax.axis_size("x")
    kinds, depth, columns = weight.shape
    hbm = pl.BlockSpec(memory_space=pl.ANY)
    return pl.pallas_call(
        norm_kernel,
        out_shape=(jax.ShapeDtypeStruct((rows, width // peers), bf16),) * peers
        + (jax.ShapeDtypeStruct((kinds, depth // 2, columns), bf16),),
        in_specs=[smem(), vmem(), vmem(), hbm],
        out_specs=(vmem(),) * peers + (hbm,),
        scratch_shapes=[pltpu.SemaphoreType.DMA],
        compiler_params=params(),
        cost_estimate=pl.CostEstimate(
            flops=6 * rows * width, bytes_accessed=4 * rows * width, transcendentals=0
        ),
        name="normalize",
    )(place, tokens, gain, weight)


def project_kernel(*refs):
    n = (len(refs) - 3) // 2
    tokens, (mine, near, far), outs = refs[:n], refs[n : n + 3], refs[n + 3 :]
    half, quarter, width = mine.shape[1], near.shape[1], mine.shape[2]
    for block, out in zip(tokens, outs, strict=True):
        for k in range(mine.shape[0]):
            total = jnp.dot(block[:, :half], mine[k], preferred_element_type=f32)
            total += jnp.dot(
                block[:, half : half + quarter], near[k], preferred_element_type=f32
            )
            total += jnp.dot(block[:, half + quarter :], far[k], preferred_element_type=f32)
            out[:, k * width : (k + 1) * width] = total.astype(out.dtype)


def project(tokens, weights):
    rows, depth = tokens[0].shape
    width = weights[0].shape[0] * weights[0].shape[2]
    n = len(tokens)
    return pl.pallas_call(
        project_kernel,
        out_shape=(jax.ShapeDtypeStruct((rows, width), f32),)
        + (jax.ShapeDtypeStruct((rows, width), bf16),) * (n - 1),
        in_specs=[vmem()] * (n + 3),
        out_specs=(vmem(),) * n,
        compiler_params=params(),
        cost_estimate=pl.CostEstimate(
            flops=2 * n * rows * depth * width,
            bytes_accessed=2 * depth * width + 2 * n * rows * depth + 4 * n * rows * width,
            transcendentals=0,
        ),
        name="project",
    )(*tokens, *weights)


def neighbour_share(share):
    yh, cores, yl = (lax.axis_size(a) for a in ("yh", "core", "yl"))
    ys = yh * yl
    moves = []
    for y in range(ys):
        for core in range(cores):
            to = (y + (1 if core == 0 else -1)) % ys
            moves.append(tuple((v // yl * cores + core) * yl + v % yl for v in (y, to)))
    return lax.ppermute(share, ("yh", "core", "yl"), moves)


def body(pseudo_grad, block_exponent, base_params, outer_momentum, tokens, norm_gain, kv_weight):
    x, yl, core = (lax.axis_index(a) for a in ("x", "yl", "core"))
    place = jnp.stack([x, yl, core]).astype(jnp.int32)
    after = lax.optimization_barrier

    keep, send = dequantize(place, pseudo_grad[0], block_exponent[0].T)
    got = shift(send, "core", 1)

    (tokens, _) = after((tokens, send))
    *blocks, share = normalize(place, tokens, norm_gain.reshape(1, -1), kv_weight)
    arrived = [blocks[0]] + [shift(block, "x", k) for k, block in enumerate(blocks) if k]
    near = neighbour_share(share)

    pair = (keep.astype(f32) + got.astype(f32)).astype(bf16)
    total = scatter_group(pair)
    total, near, *arrived = after((total, near, *arrived))
    far = shift(near, "core", 1)
    average = (sum_thirds(total) / lax.axis_size(REPLICA)).astype(bf16)

    partial = project(arrived, (kv_weight, near, far))
    average, *partial = after((average, *partial))
    average = gather_group(average)
    other = shift(average, "core", 1)

    total = partial[0]
    for k, part in enumerate(partial):
        if k:
            total = total + shift(part, "x", -k).astype(f32)
    keys_values = total.astype(bf16)

    new_params, new_momentum = update(place, average, other, base_params, outer_momentum)
    return (new_params, new_momentum, keys_values)


def solution(mesh):
    cut = Mesh(mesh.devices.reshape(SHAPE), NAMES)
    placed = (
        P(REPLICA, FSDP, None),
        P(REPLICA, FSDP, None),
        P(FSDP, None),
        P(FSDP, None),
        P((*REPLICA, *FSDP), None),
        P(),
        P(None, FSDP, None),
    )
    return jax.shard_map(
        body,
        mesh=cut,
        in_specs=placed,
        out_specs=(P(FSDP, None), P(FSDP, None), P((*REPLICA, *FSDP), None)),
        check_vma=False,
    )
```

time: 868 us -> 131 us (0.15)
  waiting for transfers between devices: 830 us -> 26.6 us
  starting transfers between devices: 0.08 us -> 59.2 us
  blocking collectives: 0 us -> 18 us
  between operations: 15.5 us -> 0.88 us
  Pallas kernels: 0 us -> 11.2 us
    psum x1 -> x0, waiting for transfers between devices: 830 us -> none  [outer_update(): average = lax.psum(delta, 'replica') / count]
    ppermute x0 -> x10, starting transfers between devices: none -> 42.2 us  [the longest x9 38.5 us: shift(): return lax.ppermute(value, axis, [(i, (i + by) % n) for i in range(n)])]
    ppermute x0 -> x10, waiting for transfers between devices: none -> 19.6 us  [the longest x9 19.6 us: shift(): return lax.ppermute(value, axis, [(i, (i + by) % n) for i in range(n)])]
    all_to_all x0 -> x1, blocking collectives: none -> 18 us  [sum_thirds(): lax.all_to_all(jnp.broadcast_to(value, (third, *value.shape)), 'zh', 0, 0...]
    all_to_all x0 -> x2, starting transfers between devices: none -> 17.1 us  [the longest x1 12.8 us: gather_group(): lax.all_to_all(jnp.broadcast_to(value, (group, *value.shape)), GROUP, 0,...]
    pallas_call x0 -> x4, Pallas kernels: none -> 11.2 us  [the longest x1 4.21 us: project(): pl.pallas_call(project_kernel, out_shape=(jax.ShapeDtypeStruct((rows, wid...]
  transfers between devices with their start and end apart: 2 -> 12, of which waited for: 1 -> 6; matrix products, arithmetic and copies ran while one was open for 1% -> 2% of each run, Pallas kernels for 0% -> 2%
where the time goes in v1:
time: 131 us; the launch traced here: 130 us
  starting transfers between devices  59.2 us (45%)
  waiting for transfers between devices  26.6 us (20%)
  blocking collectives  18 us (14%)
  Pallas kernels  11.2 us (9%)
  local copies, waits for them, and re-layouts  9.86 us (8%)
  other arithmetic  4.13 us (3%)
    ppermute x9, starting transfers between devices, shift(): return lax.ppermute(value, axis, [(i, (i + by) % n) for i in range(n)])  38.5 us
    ppermute x9, waiting for transfers between devices, shift(): return lax.ppermute(value, axis, [(i, (i + by) % n) for i in range(n)])  19.6 us
    all_to_all x1, blocking collectives, sum_thirds(): lax.all_to_all(jnp.broadcast_to(value, (third, *value.shape)), 'zh', 0, 0...  18 us
    all_to_all x1, starting transfers between devices, gather_group(): lax.all_to_all(jnp.broadcast_to(value, (group, *value.shape)), GROUP, 0,...  12.8 us
    unnamed x28, local copies, waits for them, and re-layouts  8.98 us
    all_to_all x1, waiting for transfers between devices, gather_group(): lax.all_to_all(jnp.broadcast_to(value, (group, *value.shape)), GROUP, 0,...  7 us
    all_to_all x1, starting transfers between devices, scatter_group(): parts = lax.all_to_all(parts, GROUP, 0, 0, tiled=True)  4.25 us
    pallas_call x1, Pallas kernels, project(): pl.pallas_call(project_kernel, out_shape=(jax.ShapeDtypeStruct((rows, wid...  4.21 us
  transfers between devices with their start and end apart: 12, of which 6 were waited for; matrix products, arithmetic and copies ran while one was open for 2% of the time, Pallas kernels for 2%

profile of v1, /device:TPU:1, one launch (start us, length us, event | category | flops | bytes accessed | tf_op | source)
XLA Modules:
  0.0 129.9 jit_solution(11663053254941763906)
XLA Ops:
  0.7 1.4 %copy-done.3 = bf16[1,1024,512]{2,1,0:T(8,128)(2,1)S(1)} copy-done((bf16[1,1024,512]{2,1,0:T(8,128)(2,1)S(1)}, bf16[1,1024,512]{2,1,0:T(8,128)(2,1)}, u32[]{:S(2)}) %copy-start.3) | copy-done | bytes 1048600
  2.8 1.0 dequantize.1
  3.8 12.4 %collective-permute-start = (bf16[512,512]{1,0:T(8,128)(2,1)S(1)}, bf16[512,512]{1,0:T(8,128)(2,1)S(1)}, u32[]{:S(2)}, u32[]{:S(2)}) collective-permute-start(bf16[512,512]{1,0:T(8,128)(2,1)S(1)} %get-tuple-element.29), channel_id=1, source_target_pairs={{0,8},{8,0},{1,9},{9,1},{2,10},{10,2},{3,11},{11,3},{4,12},{12,4},... | collective-permute-start | bytes 1572872 | tf_op jit(solution)/shard_map/ppermute | solution.py:37
  16.2 1.5 %collective-permute-done = bf16[512,512]{1,0:T(8,128)(2,1)S(1)} collective-permute-done((bf16[512,512]{1,0:T(8,128)(2,1)S(1)}, bf16[512,512]{1,0:T(8,128)(2,1)S(1)}, u32[]{:S(2)}, u32[]{:S(2)}) %collective-permute-start) | collective-permute-done | bytes 524320 | tf_op jit(solution)/shard_map/ppermute | solution.py:37
  17.8 0.9 add_convert_fusion
  18.7 4.2 %all-to-all-start = ((bf16[16,32,512]{2,1,0:T(8,128)(2,1)}), bf16[16,32,512]{2,1,0:T(8,128)(2,1)}, u32[]{:S(2)}, u32[]{:S(2)}) async-start(bf16[16,32,512]{2,1,0:T(8,128)(2,1)} %bitcast.6), calls=%async_computation | async-start | bytes 1048576 | tf_op jit(solution)/shard_map/all_to_all | solution.py:142
  23.0 2.9 %normalize.1 = (bf16[128,2048]{1,0:T(8,128)(2,1)S(1)}, bf16[128,2048]{1,0:T(8,128)(2,1)}, bf16[128,2048]{1,0:T(8,128)(2,1)}, bf16[128,2048]{1,0:T(8,128)(2,1)}, bf16[2,512,512]{2,1,0:T(8,128)(2,1)S(1)}) custom-call(s32[3]{0:T(128)S(1)} %pad_add_fusion.place, bf16[128,8192]{1,0:T(8,128)(2,1)S(1)} %copy-done, bf16[1,8192]{1,0:T(2,128)(2,1)S(1)} %reshape.16.gain, ...), custom_call_target="tpu_custom_call" | custom-call | flops 6291456 | bytes 4194304 | tf_op jit(solution)/shard_map/normalize/pallas_call | solution.py:190
  26.7 3.7 %collective-permute-start.1 = (bf16[2,512,512]{2,1,0:T(8,128)(2,1)S(1)}, bf16[2,512,512]{2,1,0:T(8,128)(2,1)S(1)}, u32[]{:S(2)}, u32[]{:S(2)}) collective-permute-start(bf16[2,512,512]{2,1,0:T(8,128)(2,1)S(1)} %get-tuple-element.31), channel_id=1, source_target_pairs={{0,1},{8,585},{1,192},{9,8},{192,193},{200,9},{193,384},{201,200},... | collective-permute-start | bytes 3145736 | tf_op jit(solution)/shard_map/ppermute | solution.py:247
  30.4 3.1 %collective-permute-start.2 = (bf16[128,2048]{1,0:T(8,128)(2,1)}, bf16[128,2048]{1,0:T(8,128)(2,1)S(1)}, u32[]{:S(2)}, u32[]{:S(2)}) collective-permute-start(bf16[128,2048]{1,0:T(8,128)(2,1)} %get-tuple-element.33), channel_id=1, source_target_pairs={{0,2},{2,4},{4,6},{6,0},{1,3},{3,5},{5,7},{7,1},{8,10},{10,12},{12... | collective-permute-start | bytes 1572872 | tf_op jit(solution)/shard_map/ppermute | solution.py:37
  33.6 4.4 %collective-permute-start.3 = (bf16[128,2048]{1,0:T(8,128)(2,1)}, bf16[128,2048]{1,0:T(8,128)(2,1)S(1)}, u32[]{:S(2)}, u32[]{:S(2)}) collective-permute-start(bf16[128,2048]{1,0:T(8,128)(2,1)} %get-tuple-element.34), channel_id=1, source_target_pairs={{0,4},{2,6},{4,0},{6,2},{1,5},{3,7},{5,1},{7,3},{8,12},{10,14},{12... | collective-permute-start | bytes 1572872 | tf_op jit(solution)/shard_map/ppermute | solution.py:37
  37.9 3.1 %collective-permute-start.4 = (bf16[128,2048]{1,0:T(8,128)(2,1)}, bf16[128,2048]{1,0:T(8,128)(2,1)}, u32[]{:S(2)}, u32[]{:S(2)}) collective-permute-start(bf16[128,2048]{1,0:T(8,128)(2,1)} %get-tuple-element.35), channel_id=1, source_target_pairs={{0,6},{2,0},{4,2},{6,4},{1,7},{3,1},{5,3},{7,5},{8,14},{10,8},{12,... | collective-permute-start | bytes 1572872 | tf_op jit(solution)/shard_map/ppermute | solution.py:37
  41.0 1.1 convert_reduce_fusion
  42.1 4.7 %collective-permute-done.2.refs_1_ = bf16[128,2048]{1,0:T(8,128)(2,1)S(1)} collective-permute-done((bf16[128,2048]{1,0:T(8,128)(2,1)}, bf16[128,2048]{1,0:T(8,128)(2,1)S(1)}, u32[]{:S(2)}, u32[]{:S(2)}) %collective-permute-start.2) | collective-permute-done | bytes 524320 | tf_op jit(solution)/shard_map/ppermute | solution.py:37
  46.8 0.8 copy-done.7
  47.6 11.1 %collective-permute-done.3.refs_2_ = bf16[128,2048]{1,0:T(8,128)(2,1)S(1)} collective-permute-done((bf16[128,2048]{1,0:T(8,128)(2,1)}, bf16[128,2048]{1,0:T(8,128)(2,1)S(1)}, u32[]{:S(2)}, u32[]{:S(2)}) %collective-permute-start.3) | collective-permute-done | bytes 524320 | tf_op jit(solution)/shard_map/ppermute | solution.py:37
  59.6 1.1 collective-permute-done.4.refs_3_
  60.7 2.1 %collective-permute-start.5 = (bf16[2,512,512]{2,1,0:T(8,128)(2,1)S(1)}, bf16[2,512,512]{2,1,0:T(8,128)(2,1)S(1)}, u32[]{:S(2)}, u32[]{:S(2)}) collective-permute-start(bf16[2,512,512]{2,1,0:T(8,128)(2,1)S(1)} %collective-permute-done.1.refs_5_), channel_id=1, source_target_pairs={{0,8},{8,0},{1,9},{9,1},{2,10},{10,2},{3,11},{11,3},{4,12},{12,4},... | collective-permute-start | bytes 3145736 | tf_op jit(solution)/shard_map/ppermute | solution.py:37
  62.8 18.0 %all_to_all.15 = f32[3,32,512]{2,1,0:T(8,128)S(1)} all-to-all(f32[3,32,512]{2,1,0:T(8,128)S(1)} %broadcast_in_dim.6), channel_id=1, replica_groups=mesh['yh'=4,'zh'=3,'zl'=4,'core'=2,'x'=4,'yl'=2] {'zh'}, dimensions={0} | all-to-all | bytes 393216 | tf_op jit(solution)/shard_map/all_to_all | solution.py:148
  80.9 1.0 copy-done.6
  81.9 1.0 copy-done.8
  83.0 1.0 copy-done.10
  84.0 4.2 %project.1 = (f32[128,1024]{1,0:T(8,128)S(1)}, bf16[128,1024]{1,0:T(8,128)(2,1)S(1)}, bf16[128,1024]{1,0:T(8,128)(2,1)S(1)}, bf16[128,1024]{1,0:T(8,128)(2,1)S(1)}) custom-call(bf16[128,2048]{1,0:T(8,128)(2,1)S(1)} %copy-done.6, bf16[128,2048]{1,0:T(8,128)(2,1)S(1)} %copy-done.8, bf16[128,2048]{1,0:T(8,128)(2,1)S(1)} %copy-done.10, ...), custom_call_target="tpu_custom_call" | custom-call | flops 2147483648 | bytes 8388608 | tf_op jit(solution)/shard_map/project/pallas_call | solution.py:223
  89.6 0.8 broadcast_in_dim.7
  90.5 12.8 %all-to-all-start.2 = ((bf16[16,32,512]{2,1,0:T(8,128)(2,1)}), bf16[16,32,512]{2,1,0:T(8,128)(2,1)S(1)}, u32[]{:S(2)}, u32[]{:S(2)}) async-start(bf16[16,32,512]{2,1,0:T(8,128)(2,1)} %broadcast_in_dim.7), calls=%async_computation.2 | async-start | bytes 1048576 | tf_op jit(solution)/shard_map/all_to_all | solution.py:133
  103.3 4.3 %collective-permute-start.7 = (bf16[128,1024]{1,0:T(8,128)(2,1)}, bf16[128,1024]{1,0:T(8,128)(2,1)}, u32[]{:S(2)}, u32[]{:S(2)}) collective-permute-start(bf16[128,1024]{1,0:T(8,128)(2,1)} %copy-done.12), channel_id=1, source_target_pairs={{0,6},{2,0},{4,2},{6,4},{1,7},{3,1},{5,3},{7,5},{8,14},{10,8},{12,... | collective-permute-start | bytes 786440 | tf_op jit(solution)/shard_map/ppermute | solution.py:37
  107.6 3.4 %collective-permute-start.8 = (bf16[128,1024]{1,0:T(8,128)(2,1)}, bf16[128,1024]{1,0:T(8,128)(2,1)}, u32[]{:S(2)}, u32[]{:S(2)}) collective-permute-start(bf16[128,1024]{1,0:T(8,128)(2,1)} %copy-done.11), channel_id=1, source_target_pairs={{0,4},{2,6},{4,0},{6,2},{1,5},{3,7},{5,1},{7,3},{8,12},{10,14},{12... | collective-permute-start | bytes 786440 | tf_op jit(solution)/shard_map/ppermute | solution.py:37
  111.0 1.9 %collective-permute-start.9 = (bf16[128,1024]{1,0:T(8,128)(2,1)S(1)}, bf16[128,1024]{1,0:T(8,128)(2,1)}, u32[]{:S(2)}, u32[]{:S(2)}) collective-permute-start(bf16[128,1024]{1,0:T(8,128)(2,1)S(1)} %get-tuple-element.52), channel_id=1, source_target_pairs={{0,2},{2,4},{4,6},{6,0},{1,3},{3,5},{5,7},{7,1},{8,10},{10,12},{12... | collective-permute-start | bytes 786440 | tf_op jit(solution)/shard_map/ppermute | solution.py:37
  113.0 7.0 %all-to-all-done.2 = bf16[16,32,512]{2,1,0:T(8,128)(2,1)S(1)} async-done(((bf16[16,32,512]{2,1,0:T(8,128)(2,1)}), bf16[16,32,512]{2,1,0:T(8,128)(2,1)S(1)}, u32[]{:S(2)}, u32[]{:S(2)}) %all-to-all-start.2) | async-done | bytes 524320 | tf_op jit(solution)/shard_map/all_to_all | solution.py:133
  120.0 3.8 %collective-permute-start.6 = (bf16[512,512]{1,0:T(8,128)(2,1)S(1)}, bf16[512,512]{1,0:T(8,128)(2,1)S(1)}, u32[]{:S(2)}, u32[]{:S(2)}) collective-permute-start(bf16[512,512]{1,0:T(8,128)(2,1)S(1)} %bitcast.9), channel_id=1, source_target_pairs={{0,8},{8,0},{1,9},{9,1},{2,10},{10,2},{3,11},{11,3},{4,12},{12,4},... | collective-permute-start | bytes 1572872 | tf_op jit(solution)/shard_map/ppermute | solution.py:37
  123.8 1.1 collective-permute-done.9
  124.9 2.0 %add_convert_fusion.1 = bf16[128,1024]{1,0:T(8,128)(2,1)} fusion(bf16[128,1024]{1,0:T(8,128)(2,1)} %collective-permute-done.9, bf16[128,1024]{1,0:T(8,128)(2,1)} %collective-permute-done.8, f32[128,1024]{1,0:T(8,128)S(1)} %get-tuple-element.49, bf16[128,1024]{1,0:T(8,128)(2,1)} %collective-permute-done.7), kind=kLoop, calls=%fused_computation.2 | loop fusion | flops 917504 | bytes 1572864 | tf_op jit(solution)/shard_map/convert_element_type | solution.py:278
  126.9 3.0 %update.1 = (bf16[1024,512]{1,0:T(8,128)(2,1)}, f32[1024,512]{1,0:T(8,128)}) custom-call(s32[3]{0:T(128)S(1)} %pad_add_fusion.place, bf16[512,512]{1,0:T(8,128)(2,1)S(1)} %bitcast.10, bf16[512,512]{1,0:T(8,128)(2,1)S(1)} %collective-permute-done.6.other, bf16[1024,512]{1,0:T(8,128)(2,1)S(1)} %copy-done.2, f32[1024,512]{1,0:T(8,128)S(1)} %copy-done.1), custom_call_target="tpu_custom_call" | custom-call | flops 4194304 | bytes 7340032 | tf_op jit(solution)/shard_map/update/pallas_call | solution.py:106
  (34 shorter events, 3.9 us)
Async XLA Ops:
  0.6 22.4 %copy-start = (bf16[128,8192]{1,0:T(8,128)(2,1)S(1)}, bf16[128,8192]{1,0:T(8,128)(2,1)}, u32[]{:S(2)}) copy-start(bf16[128,8192]{1,0:T(8,128)(2,1)} %tokens) | copy-start | bytes 6291460
  0.7 1.4 %copy-start.3 = (bf16[1,1024,512]{2,1,0:T(8,128)(2,1)S(1)}, bf16[1,1024,512]{2,1,0:T(8,128)(2,1)}, u32[]{:S(2)}) copy-start(bf16[1,1024,512]{2,1,0:T(8,128)(2,1)} %param.7) | copy-start | bytes 3145732
  2.1 0.7 copy-start.4
  2.8 20.1 %copy-start.13 = (bf16[8192]{0:T(1024)(128)(2,1)S(1)}, bf16[8192]{0:T(1024)(128)(2,1)}, u32[]{:S(2)}) copy-start(bf16[8192]{0:T(1024)(128)(2,1)} %param.12) | copy-start | bytes 49156
  3.8 13.9 %collective-permute-start = (bf16[512,512]{1,0:T(8,128)(2,1)S(1)}, bf16[512,512]{1,0:T(8,128)(2,1)S(1)}, u32[]{:S(2)}, u32[]{:S(2)}) collective-permute-start(bf16[512,512]{1,0:T(8,128)(2,1)S(1)} %get-tuple-element.29), channel_id=1, source_target_pairs={{0,8},{8,0},{1,9},{9,1},{2,10},{10,2},{3,11},{11,3},{4,12},{12,4},... | collective-permute-start | bytes 1572872 | tf_op jit(solution)/shard_map/ppermute | solution.py:37
  18.7 22.3 %all-to-all-start = ((bf16[16,32,512]{2,1,0:T(8,128)(2,1)}), bf16[16,32,512]{2,1,0:T(8,128)(2,1)}, u32[]{:S(2)}, u32[]{:S(2)}) async-start(bf16[16,32,512]{2,1,0:T(8,128)(2,1)} %bitcast.6), calls=%async_computation | async-start | bytes 1048576 | tf_op jit(solution)/shard_map/all_to_all | solution.py:142
  25.9 0.8 copy-start.5
  26.7 34.0 %collective-permute-start.1 = (bf16[2,512,512]{2,1,0:T(8,128)(2,1)S(1)}, bf16[2,512,512]{2,1,0:T(8,128)(2,1)S(1)}, u32[]{:S(2)}, u32[]{:S(2)}) collective-permute-start(bf16[2,512,512]{2,1,0:T(8,128)(2,1)S(1)} %get-tuple-element.31), channel_id=1, source_target_pairs={{0,1},{8,585},{1,192},{9,8},{192,193},{200,9},{193,384},{201,200},... | collective-permute-start | bytes 3145736 | tf_op jit(solution)/shard_map/ppermute | solution.py:247
  30.4 16.4 %collective-permute-start.2 = (bf16[128,2048]{1,0:T(8,128)(2,1)}, bf16[128,2048]{1,0:T(8,128)(2,1)S(1)}, u32[]{:S(2)}, u32[]{:S(2)}) collective-permute-start(bf16[128,2048]{1,0:T(8,128)(2,1)} %get-tuple-element.33), channel_id=1, source_target_pairs={{0,2},{2,4},{4,6},{6,0},{1,3},{3,5},{5,7},{7,1},{8,10},{10,12},{12... | collective-permute-start | bytes 1572872 | tf_op jit(solution)/shard_map/ppermute | solution.py:37
  33.6 25.2 %collective-permute-start.3 = (bf16[128,2048]{1,0:T(8,128)(2,1)}, bf16[128,2048]{1,0:T(8,128)(2,1)S(1)}, u32[]{:S(2)}, u32[]{:S(2)}) collective-permute-start(bf16[128,2048]{1,0:T(8,128)(2,1)} %get-tuple-element.34), channel_id=1, source_target_pairs={{0,4},{2,6},{4,0},{6,2},{1,5},{3,7},{5,1},{7,3},{8,12},{10,14},{12... | collective-permute-start | bytes 1572872 | tf_op jit(solution)/shard_map/ppermute | solution.py:37
  37.9 22.8 %collective-permute-start.4 = (bf16[128,2048]{1,0:T(8,128)(2,1)}, bf16[128,2048]{1,0:T(8,128)(2,1)}, u32[]{:S(2)}, u32[]{:S(2)}) collective-permute-start(bf16[128,2048]{1,0:T(8,128)(2,1)} %get-tuple-element.35), channel_id=1, source_target_pairs={{0,6},{2,0},{4,2},{6,4},{1,7},{3,1},{5,3},{7,5},{8,14},{10,8},{12,... | collective-permute-start | bytes 1572872 | tf_op jit(solution)/shard_map/ppermute | solution.py:37
  46.8 0.8 copy-start.7
  58.8 0.8 copy-start.9
  60.7 20.2 %collective-permute-start.5 = (bf16[2,512,512]{2,1,0:T(8,128)(2,1)S(1)}, bf16[2,512,512]{2,1,0:T(8,128)(2,1)S(1)}, u32[]{:S(2)}, u32[]{:S(2)}) collective-permute-start(bf16[2,512,512]{2,1,0:T(8,128)(2,1)S(1)} %collective-permute-done.1.refs_5_), channel_id=1, source_target_pairs={{0,8},{8,0},{1,9},{9,1},{2,10},{10,2},{3,11},{11,3},{4,12},{12,4},... | collective-permute-start | bytes 3145736 | tf_op jit(solution)/shard_map/ppermute | solution.py:37
  80.9 1.0 copy-start.6
  81.9 1.0 copy-start.8
  83.0 1.0 copy-start.10
  88.2 0.7 copy-start.11
  88.9 0.7 copy-start.12
  89.6 37.3 %copy-start.1 = (f32[1024,512]{1,0:T(8,128)S(1)}, f32[1024,512]{1,0:T(8,128)}, u32[]{:S(2)}) copy-start(f32[1024,512]{1,0:T(8,128)} %momentum.1) | copy-start | bytes 6291460
  90.5 29.5 %all-to-all-start.2 = ((bf16[16,32,512]{2,1,0:T(8,128)(2,1)}), bf16[16,32,512]{2,1,0:T(8,128)(2,1)S(1)}, u32[]{:S(2)}, u32[]{:S(2)}) async-start(bf16[16,32,512]{2,1,0:T(8,128)(2,1)} %broadcast_in_dim.7), calls=%async_computation.2 | async-start | bytes 1048576 | tf_op jit(solution)/shard_map/all_to_all | solution.py:133
  103.3 20.5 %collective-permute-start.7 = (bf16[128,1024]{1,0:T(8,128)(2,1)}, bf16[128,1024]{1,0:T(8,128)(2,1)}, u32[]{:S(2)}, u32[]{:S(2)}) collective-permute-start(bf16[128,1024]{1,0:T(8,128)(2,1)} %copy-done.12), channel_id=1, source_target_pairs={{0,6},{2,0},{4,2},{6,4},{1,7},{3,1},{5,3},{7,5},{8,14},{10,8},{12,... | collective-permute-start | bytes 786440 | tf_op jit(solution)/shard_map/ppermute | solution.py:37
  107.6 16.2 %collective-permute-start.8 = (bf16[128,1024]{1,0:T(8,128)(2,1)}, bf16[128,1024]{1,0:T(8,128)(2,1)}, u32[]{:S(2)}, u32[]{:S(2)}) collective-permute-start(bf16[128,1024]{1,0:T(8,128)(2,1)} %copy-done.11), channel_id=1, source_target_pairs={{0,4},{2,6},{4,0},{6,2},{1,5},{3,7},{5,1},{7,3},{8,12},{10,14},{12... | collective-permute-start | bytes 786440 | tf_op jit(solution)/shard_map/ppermute | solution.py:37
  111.0 13.9 %collective-permute-start.9 = (bf16[128,1024]{1,0:T(8,128)(2,1)S(1)}, bf16[128,1024]{1,0:T(8,128)(2,1)}, u32[]{:S(2)}, u32[]{:S(2)}) collective-permute-start(bf16[128,1024]{1,0:T(8,128)(2,1)S(1)} %get-tuple-element.52), channel_id=1, source_target_pairs={{0,2},{2,4},{4,6},{6,0},{1,3},{3,5},{5,7},{7,1},{8,10},{10,12},{12... | collective-permute-start | bytes 786440 | tf_op jit(solution)/shard_map/ppermute | solution.py:37
  120.0 6.9 %copy-start.2 = (bf16[1024,512]{1,0:T(8,128)(2,1)S(1)}, bf16[1024,512]{1,0:T(8,128)(2,1)}, u32[]{:S(2)}) copy-start(bf16[1024,512]{1,0:T(8,128)(2,1)} %base.1) | copy-start | bytes 3145732
  120.0 6.9 %collective-permute-start.6 = (bf16[512,512]{1,0:T(8,128)(2,1)S(1)}, bf16[512,512]{1,0:T(8,128)(2,1)S(1)}, u32[]{:S(2)}, u32[]{:S(2)}) collective-permute-start(bf16[512,512]{1,0:T(8,128)(2,1)S(1)} %bitcast.9), channel_id=1, source_target_pairs={{0,8},{8,0},{1,9},{9,1},{2,10},{10,2},{3,11},{11,3},{4,12},{12,4},... | collective-permute-start | bytes 1572872 | tf_op jit(solution)/shard_map/ppermute | solution.py:37

commit v2 on v1

--- a/solution.py
+++ b/solution.py
@@ -37,40 +37,106 @@
     return lax.ppermute(value, axis, [(i, (i + by) % n) for i in range(n)])
 
 
-def dequantize_kernel(place, values, exponents, keep, send):
-    half, width = keep.shape
-    blocks = exponents.shape[0]
-    core = place[2]
-    scale = jnp.exp2(exponents[...].astype(f32))
-    lane = lax.broadcasted_iota(jnp.int32, (blocks, width), 1)
-    row = lax.broadcasted_iota(jnp.int32, (blocks, width), 0)
-    spread = jnp.where(lane // (width // blocks) == row, 1.0, 0.0).astype(f32)
-    for out, part in ((keep, core), (send, 1 - core)):
-        start = pl.multiple_of(part * half, half)
-        mine = jnp.where(part == 0, scale[:, :half], scale[:, half:])
-        wide = lax.dot_general(
-            mine.astype(bf16),
-            spread.astype(bf16),
-            (((0,), (0,)), ((), ())),
-            preferred_element_type=f32,
-        )
-        out[...] = (values[pl.ds(start, half), :].astype(f32) * wide).astype(bf16)
-
-
-def dequantize(place, values, exponents):
-    rows, width = values.shape
-    half = jax.ShapeDtypeStruct((rows // 2, width), bf16)
+def hbm():
+    return pl.BlockSpec(memory_space=pl.ANY)
+
+
+def front_kernel(place, gain, exponents, tokens, values, weight, *refs):
+    (*blocks, keep, send, share), scratch = refs[: -len(FRONT)], refs[-len(FRONT) :]
+    x, yl, core = place[0], place[1], place[2]
+    held, normed, delta, dequantized, token_in, block_out, delta_in, delta_out, moved = scratch
+    peers, rows, block = normed.shape
+    half, quarter = block // 2, block // 4
+
+    def chunk(i):
+        at = pl.ds(i * block, block)
+        return pltpu.make_async_copy(tokens.at[:, at], held.at[:, at], token_in.at[i])
+
+    for i in range(peers):
+        chunk(i).start()
+    delta_copy = pltpu.make_async_copy(values, delta, delta_in)
+    delta_copy.start()
+    depth = share.shape[1]
+    mine = pl.ds(pl.multiple_of(core * depth, depth), depth)
+    share_copy = pltpu.make_async_copy(weight.at[:, mine, :], share, moved)
+    share_copy.start()
+
+    total = jnp.zeros((rows, 128), f32)
+    for i in range(peers):
+        chunk(i).wait()
+        for at in range(i * block, (i + 1) * block, 128):
+            piece = held[:, at : at + 128].astype(f32)
+            total += piece * piece
+    meansq = jnp.sum(total, axis=1, keepdims=True) / (peers * block)
+    scale = lax.rsqrt(meansq + 1e-05)
+    outs = []
+    for k in (*range(1, peers), 0):
+        first = lax.rem(x + k, peers) * block
+        for at, start, size in (
+            (0, yl * half, half),
+            (half, (1 - yl) * half + core * quarter, quarter),
+            (half + quarter, (1 - yl) * half + (1 - core) * quarter, quarter),
+        ):
+            columns = pl.ds(pl.multiple_of(first + start, quarter), size)
+            piece = held[:, columns].astype(f32) * scale * gain[:, columns].astype(f32)
+            normed[k, :, at : at + size] = piece.astype(bf16)
+        outs.append(pltpu.make_async_copy(normed.at[k], blocks[k], block_out.at[k]))
+        outs[-1].start()
+
+    near, width = keep.shape
+    count = exponents.shape[0]
+    power = jnp.exp2(exponents[...].astype(f32))
+    lane = lax.broadcasted_iota(jnp.int32, (count, width), 1)
+    row = lax.broadcasted_iota(jnp.int32, (count, width), 0)
+    spread = jnp.where(lane // (width // count) == row, 1.0, 0.0).astype(bf16)
+    delta_copy.wait()
+    for i, (out, part) in enumerate(((send, 1 - core), (keep, core))):
+        start = pl.multiple_of(part * near, near)
+        own = jnp.where(part == 0, power[:, :near], power[:, near:]).astype(bf16)
+        wide = lax.dot_general(own, spread, (((0,), (0,)), ((), ())), preferred_element_type=f32)
+        dequantized[i] = (delta[pl.ds(start, near), :].astype(f32) * wide).astype(bf16)
+        outs.append(pltpu.make_async_copy(dequantized.at[i], out, delta_out.at[i]))
+        outs[-1].start()
+    for copy in (*outs, share_copy):
+        copy.wait()
+
+
+FRONT = ("held", "normed", "delta", "dequantized", "in", "out", "din", "dout", "moved")
+
+
+def front(place, tokens, gain, values, exponents, weight):
+    rows, width = tokens.shape
+    peers = lax.axis_size("x")
+    block = width // peers
+    deep, across = values.shape
+    kinds, depth, columns = weight.shape
+    dma = pltpu.SemaphoreType.DMA
     return pl.pallas_call(
-        dequantize_kernel,
-        out_shape=(half, half),
-        in_specs=[smem(), vmem(), vmem()],
-        out_specs=(vmem(), vmem()),
+        front_kernel,
+        out_shape=(jax.ShapeDtypeStruct((rows, block), bf16),) * peers
+        + (jax.ShapeDtypeStruct((deep // 2, across), bf16),) * 2
+        + (jax.ShapeDtypeStruct((kinds, depth // 2, columns), bf16),),
+        in_specs=[smem(), vmem(), vmem(), hbm(), hbm(), hbm()],
+        out_specs=(hbm(),) * (peers + 3),
+        scratch_shapes=[
+            pltpu.VMEM((rows, width), bf16),
+            pltpu.VMEM((peers, rows, block), bf16),
+            pltpu.VMEM((deep, across), bf16),
+            pltpu.VMEM((2, deep // 2, across), bf16),
+            dma((peers,)),
+            dma((peers,)),
+            dma,
+            dma((2,)),
+            dma,
+        ],
         compiler_params=params(),
         cost_estimate=pl.CostEstimate(
-            flops=4 * rows * width, bytes_accessed=4 * rows * width, transcendentals=0
-        ),
-        name="dequantize",
-    )(place, values, exponents)
+            flops=6 * rows * width + 4 * deep * across,
+            bytes_accessed=4 * rows * width + 4 * deep * across,
+            transcendentals=0,
+        ),
+        name="front",
+    )(place, gain, exponents, tokens, values, weight)
 
 
 def update_kernel(place, own, other, base, momentum, new_params, new_momentum):
@@ -151,81 +217,61 @@
     return jnp.sum(whole, axis=0)
 
 
-def norm_kernel(place, tokens, gain, weight, *refs):
-    outs, share, done = refs[:-2], refs[-2], refs[-1]
-    x, yl, core = place[0], place[1], place[2]
-    rows = share.shape[1]
-    copy = pltpu.make_async_copy(
-        weight.at[:, pl.ds(pl.multiple_of(core * rows, rows), rows), :], share, done
-    )
-    copy.start()
-    peers = len(outs)
-    width = tokens.shape[1]
-    block = width // peers
-    half, quarter = block // 2, block // 4
-    total = jnp.zeros((tokens.shape[0], 128), f32)
-    for at in range(0, width, 128):
-        piece = tokens[:, at : at + 128].astype(f32)
-        total += piece * piece
-    meansq = jnp.sum(total, axis=1, keepdims=True) / width
-    scale = lax.rsqrt(meansq + 1e-05)
-    for k, out in enumerate(outs):
-        first = lax.rem(x + k, peers) * block
-        for at, start, size in (
-            (0, yl * half, half),
-            (half, (1 - yl) * half + core * quarter, quarter),
-            (half + quarter, (1 - yl) * half + (1 - core) * quarter, quarter),
-        ):
-            columns = pl.ds(pl.multiple_of(first + start, quarter), size)
-            piece = tokens[:, columns].astype(f32) * scale * gain[:, columns].astype(f32)
-            out[:, at : at + size] = piece.astype(bf16)
-    copy.wait()
-
-
-def normalize(place, tokens, gain, weight):
-    rows, width = tokens.shape
-    peers = lax.axis_size("x")
-    kinds, depth, columns = weight.shape
-    hbm = pl.BlockSpec(memory_space=pl.ANY)
-    return pl.pallas_call(
-        norm_kernel,
-        out_shape=(jax.ShapeDtypeStruct((rows, width // peers), bf16),) * peers
-        + (jax.ShapeDtypeStruct((kinds, depth // 2, columns), bf16),),
-        in_specs=[smem(), vmem(), vmem(), hbm],
-        out_specs=(vmem(),) * peers + (hbm,),
-        scratch_shapes=[pltpu.SemaphoreType.DMA],
-        compiler_params=params(),
-        cost_estimate=pl.CostEstimate(
-            flops=6 * rows * width, bytes_accessed=4 * rows * width, transcendentals=0
-        ),
-        name="normalize",
-    )(place, tokens, gain, weight)
-
-
 def project_kernel(*refs):
-    n = (len(refs) - 3) // 2
-    tokens, (mine, near, far), outs = refs[:n], refs[n : n + 3], refs[n + 3 :]
+    ins, outs, scratch = refs[:7], refs[7:-7], refs[-7:]
+    *blocks, mine, near, far = ins
+    held, whole, first, rest, block_in, weight_in, out_sem = scratch
     half, quarter, width = mine.shape[1], near.shape[1], mine.shape[2]
-    for block, out in zip(tokens, outs, strict=True):
-        for k in range(mine.shape[0]):
-            total = jnp.dot(block[:, :half], mine[k], preferred_element_type=f32)
-            total += jnp.dot(
-                block[:, half : half + quarter], near[k], preferred_element_type=f32
-            )
-            total += jnp.dot(block[:, half + quarter :], far[k], preferred_element_type=f32)
-            out[:, k * width : (k + 1) * width] = total.astype(out.dtype)
+    copies = []
+    for i, (part, at, size) in enumerate(
+        ((mine, 0, half), (near, half, quarter), (far, half + quarter, quarter))
+    ):
+        copies.append(
+            pltpu.make_async_copy(part, whole.at[:, at : at + size, :], weight_in.at[i])
+        )
+    order = (*range(1, len(blocks)), 0)
+    arrivals = {
+        k: pltpu.make_async_copy(blocks[k], held.at[k], block_in.at[k]) for k in order
+    }
+    for copy in (*copies, *arrivals.values()):
+        copy.start()
+    for copy in copies:
+        copy.wait()
+    leaving = []
+    for k in order:
+        arrivals[k].wait()
+        out = rest.at[k - 1] if k else first
+        for kind in range(mine.shape[0]):
+            out[:, kind * width : (kind + 1) * width] = jnp.dot(
+                held[k], whole[kind], preferred_element_type=f32
+            ).astype(out.dtype)
+        leaving.append(pltpu.make_async_copy(out, outs[k], out_sem.at[k]))
+        leaving[-1].start()
+    for copy in leaving:
+        copy.wait()
 
 
 def project(tokens, weights):
     rows, depth = tokens[0].shape
-    width = weights[0].shape[0] * weights[0].shape[2]
+    kinds, _, columns = weights[0].shape
+    width = kinds * columns
     n = len(tokens)
+    dma = pltpu.SemaphoreType.DMA
     return pl.pallas_call(
         project_kernel,
         out_shape=(jax.ShapeDtypeStruct((rows, width), f32),)
         + (jax.ShapeDtypeStruct((rows, width), bf16),) * (n - 1),
-        in_specs=[vmem()] * (n + 3),
-        out_specs=(vmem(),) * n,
+        in_specs=[hbm()] * (n + 3),
+        out_specs=(hbm(),) * n,
+        scratch_shapes=[
+            pltpu.VMEM((n, rows, depth), bf16),
+            pltpu.VMEM((kinds, depth, columns), bf16),
+            pltpu.VMEM((rows, width), f32),
+            pltpu.VMEM((n - 1, rows, width), bf16),
+            dma((n,)),
+            dma((3,)),
+            dma((n,)),
+        ],
         compiler_params=params(),
         cost_estimate=pl.CostEstimate(
             flops=2 * n * rows * depth * width,
@@ -252,17 +298,15 @@
     place = jnp.stack([x, yl, core]).astype(jnp.int32)
     after = lax.optimization_barrier
 
-    keep, send = dequantize(place, pseudo_grad[0], block_exponent[0].T)
-    got = shift(send, "core", 1)
-
-    (tokens, _) = after((tokens, send))
-    *blocks, share = normalize(place, tokens, norm_gain.reshape(1, -1), kv_weight)
+    *blocks, keep, send, share = front(
+        place, tokens, norm_gain.reshape(1, -1), pseudo_grad[0], block_exponent[0].T, kv_weight
+    )
     arrived = [blocks[0]] + [shift(block, "x", k) for k, block in enumerate(blocks) if k]
     near = neighbour_share(share)
+    got = shift(send, "core", 1)
 
     pair = (keep.astype(f32) + got.astype(f32)).astype(bf16)
     total = scatter_group(pair)
-    total, near, *arrived = after((total, near, *arrived))
     far = shift(near, "core", 1)
     average = (sum_thirds(total) / lax.axis_size(REPLICA)).astype(bf16)
 

time: 131 us -> 121 us (0.924)
  blocking collectives: 18 us -> 0 us
  waiting for transfers between devices: 26.6 us -> 42.5 us
  starting transfers between devices: 59.2 us -> 54.2 us
  local copies, waits for them, and re-layouts: 9.86 us -> 5.64 us
    ppermute x1, waiting for transfers between devices: 0.01 us -> 19.2 us  [neighbour_share(): return lax.ppermute(share, ('yh', 'core', 'yl'), moves)]
    all_to_all x1 -> x0, blocking collectives: 18 us -> none  [sum_thirds(): lax.all_to_all(jnp.broadcast_to(value, (third, *value.shape)), 'zh', 0, 0...]
    all_to_all x1, starting transfers between devices: 12.8 us -> 3.57 us  [gather_group(): lax.all_to_all(jnp.broadcast_to(value, (group, *value.shape)), GROUP, 0,...]
    all_to_all x0 -> x1, starting transfers between devices: none -> 5.67 us  [sum_thirds(): lax.all_to_all(jnp.broadcast_to(value, (third, *value.shape)), 'zh', 0, 0...]
    unnamed x28 -> x16, local copies, waits for them, and re-layouts: 8.98 us -> 3.36 us
    ppermute x9, waiting for transfers between devices: 19.6 us -> 16.6 us  [shift(): return lax.ppermute(value, axis, [(i, (i + by) % n) for i in range(n)])]
    ppermute x1, starting transfers between devices: 3.68 us -> 1.92 us  [neighbour_share(): return lax.ppermute(share, ('yh', 'core', 'yl'), moves)]
    pallas_call x2 -> x1, Pallas kernels: 3.95 us -> 3.72 us  [front(): pl.pallas_call(front_kernel, out_shape=(jax.ShapeDtypeStruct((rows, block...]
  transfers between devices with their start and end apart: 12 -> 13, of which waited for: 6 -> 5; matrix products, arithmetic and copies ran while one was open for 2% -> 4% of each run, Pallas kernels for 2% -> 4%
where the time goes in v2:
time: 121 us; the launch traced here: 120 us
  starting transfers between devices  54.2 us (45%)
  waiting for transfers between devices  42.5 us (35%)
  Pallas kernels  11.5 us (10%)
  local copies, waits for them, and re-layouts  5.64 us (5%)
  other arithmetic  5.22 us (4%)
    ppermute x9, starting transfers between devices, shift(): return lax.ppermute(value, axis, [(i, (i + by) % n) for i in range(n)])  38.8 us
    ppermute x1, waiting for transfers between devices, neighbour_share(): return lax.ppermute(share, ('yh', 'core', 'yl'), moves)  19.2 us
    ppermute x9, waiting for transfers between devices, shift(): return lax.ppermute(value, axis, [(i, (i + by) % n) for i in range(n)])  16.6 us
    all_to_all x1, waiting for transfers between devices, gather_group(): lax.all_to_all(jnp.broadcast_to(value, (group, *value.shape)), GROUP, 0,...  6.69 us
    all_to_all x1, starting transfers between devices, sum_thirds(): lax.all_to_all(jnp.broadcast_to(value, (third, *value.shape)), 'zh', 0, 0...  5.67 us
    pallas_call x1, Pallas kernels, project(): pl.pallas_call(project_kernel, out_shape=(jax.ShapeDtypeStruct((rows, wid...  4.77 us
    all_to_all x1, starting transfers between devices, scatter_group(): parts = lax.all_to_all(parts, GROUP, 0, 0, tiled=True)  4.24 us
    pallas_call x1, Pallas kernels, front(): pl.pallas_call(front_kernel, out_shape=(jax.ShapeDtypeStruct((rows, block...  3.72 us
  transfers between devices with their start and end apart: 13, of which 5 were waited for; matrix products, arithmetic and copies ran while one was open for 4% of the time, Pallas kernels for 4%

profile of v2, /device:TPU:1, one launch (start us, length us, event | category | flops | bytes accessed | tf_op | source)
XLA Modules:
  0.0 119.9 jit_solution(5075625806890769996)
XLA Ops:
  0.6 0.7 reshape.15.gain
  1.5 1.2 %copy-done.2 = bf16[1,1024,512]{2,1,0:T(8,128)(2,1)S(1)} copy-done((bf16[1,1024,512]{2,1,0:T(8,128)(2,1)S(1)}, bf16[1,1024,512]{2,1,0:T(8,128)(2,1)}, u32[]{:S(2)}) %copy-start.2) | copy-done | bytes 1048600
  2.7 0.7 copy-done.3
  3.4 3.7 %front.1 = (bf16[128,2048]{1,0:T(8,128)(2,1)S(1)}, bf16[128,2048]{1,0:T(8,128)(2,1)S(1)}, bf16[128,2048]{1,0:T(8,128)(2,1)S(1)}, bf16[128,2048]{1,0:T(8,128)(2,1...) custom-call(s32[3]{0:T(128)S(1)} %pad_add_fusion.place, ...), custom_call_target="tpu_custom_call" | custom-call | flops 8388608 | bytes 6291456 | tf_op jit(solution)/shard_map/front/pallas_call | solution.py:114
  7.2 12.4 %collective-permute-start = (bf16[512,512]{1,0:T(8,128)(2,1)S(1)}, bf16[512,512]{1,0:T(8,128)(2,1)S(1)}, u32[]{:S(2)}, u32[]{:S(2)}) collective-permute-start(bf16[512,512]{1,0:T(8,128)(2,1)S(1)} %get-tuple-element.22), channel_id=1, source_target_pairs={{0,8},{8,0},{1,9},{9,1},{2,10},{10,2},{3,11},{11,3},{4,12},{12,4},... | collective-permute-start | bytes 1572872 | tf_op jit(solution)/shard_map/ppermute | solution.py:37
  19.6 1.9 %collective-permute-start.4 = (bf16[2,512,512]{2,1,0:T(8,128)(2,1)S(1)}, bf16[2,512,512]{2,1,0:T(8,128)(2,1)S(1)}, u32[]{:S(2)}, u32[]{:S(2)}) collective-permute-start(bf16[2,512,512]{2,1,0:T(8,128)(2,1)S(1)} %get-tuple-element.27), channel_id=1, source_target_pairs={{0,1},{8,585},{1,192},{9,8},{192,193},{200,9},{193,384},{201,200},... | collective-permute-start | bytes 3145736 | tf_op jit(solution)/shard_map/ppermute | solution.py:293
  21.5 0.9 add_convert_fusion
  22.5 4.2 %all-to-all-start = ((bf16[16,32,512]{2,1,0:T(8,128)(2,1)}), bf16[16,32,512]{2,1,0:T(8,128)(2,1)}, u32[]{:S(2)}, u32[]{:S(2)}) async-start(bf16[16,32,512]{2,1,0:T(8,128)(2,1)} %bitcast.13), calls=%async_computation | async-start | bytes 1048576 | tf_op jit(solution)/shard_map/all_to_all | solution.py:208
  26.7 19.2 %collective-permute-done.4.refs_5_ = bf16[2,512,512]{2,1,0:T(8,128)(2,1)S(1)} collective-permute-done((bf16[2,512,512]{2,1,0:T(8,128)(2,1)S(1)}, bf16[2,512,512]{2,1,0:T(8,128)(2,1)S(1)}, u32[]{:S(2)}, u32[]{:S(2)}) %collective-permute-start.4) | collective-permute-done | bytes 1048608 | tf_op jit(solution)/shard_map/ppermute | solution.py:293
  45.9 4.3 %collective-permute-start.5 = (bf16[2,512,512]{2,1,0:T(8,128)(2,1)S(1)}, bf16[2,512,512]{2,1,0:T(8,128)(2,1)S(1)}, u32[]{:S(2)}, u32[]{:S(2)}) collective-permute-start(bf16[2,512,512]{2,1,0:T(8,128)(2,1)S(1)} %collective-permute-done.4.refs_5_), channel_id=1, source_target_pairs={{0,8},{8,0},{1,9},{9,1},{2,10},{10,2},{3,11},{11,3},{4,12},{12,4},... | collective-permute-start | bytes 3145736 | tf_op jit(solution)/shard_map/ppermute | solution.py:37
  50.3 1.9 %collective-permute-start.1 = (bf16[128,2048]{1,0:T(8,128)(2,1)}, bf16[128,2048]{1,0:T(8,128)(2,1)}, u32[]{:S(2)}, u32[]{:S(2)}) collective-permute-start(bf16[128,2048]{1,0:T(8,128)(2,1)} %copy-done.5), channel_id=1, source_target_pairs={{0,2},{2,4},{4,6},{6,0},{1,3},{3,5},{5,7},{7,1},{8,10},{10,12},{12... | collective-permute-start | bytes 1572872 | tf_op jit(solution)/shard_map/ppermute | solution.py:37
  52.2 1.9 %collective-permute-start.2 = (bf16[128,2048]{1,0:T(8,128)(2,1)}, bf16[128,2048]{1,0:T(8,128)(2,1)}, u32[]{:S(2)}, u32[]{:S(2)}) collective-permute-start(bf16[128,2048]{1,0:T(8,128)(2,1)} %copy-done.4), channel_id=1, source_target_pairs={{0,4},{2,6},{4,0},{6,2},{1,5},{3,7},{5,1},{7,3},{8,12},{10,14},{12... | collective-permute-start | bytes 1572872 | tf_op jit(solution)/shard_map/ppermute | solution.py:37
  54.1 4.6 %collective-permute-start.3 = (bf16[128,2048]{1,0:T(8,128)(2,1)S(1)}, bf16[128,2048]{1,0:T(8,128)(2,1)}, u32[]{:S(2)}, u32[]{:S(2)}) collective-permute-start(bf16[128,2048]{1,0:T(8,128)(2,1)S(1)} %get-tuple-element.26), channel_id=1, source_target_pairs={{0,6},{2,0},{4,2},{6,4},{1,7},{3,1},{5,3},{7,5},{8,14},{10,8},{12,... | collective-permute-start | bytes 1572872 | tf_op jit(solution)/shard_map/ppermute | solution.py:37
  58.7 1.1 convert_reduce_fusion
  59.9 0.7 broadcast_in_dim.6
  60.6 5.7 %all-to-all-start.1 = ((f32[3,32,512]{2,1,0:T(8,128)}), f32[3,32,512]{2,1,0:T(8,128)}, u32[]{:S(2)}, u32[]{:S(2)}) async-start(f32[3,32,512]{2,1,0:T(8,128)} %broadcast_in_dim.6), calls=%async_computation.1 | async-start | bytes 393216 | tf_op jit(solution)/shard_map/all_to_all | solution.py:214
  66.2 12.3 %collective-permute-done.1.refs_1_ = bf16[128,2048]{1,0:T(8,128)(2,1)} collective-permute-done((bf16[128,2048]{1,0:T(8,128)(2,1)}, bf16[128,2048]{1,0:T(8,128)(2,1)}, u32[]{:S(2)}, u32[]{:S(2)}) %collective-permute-start.1) | collective-permute-done | bytes 524320 | tf_op jit(solution)/shard_map/ppermute | solution.py:37
  78.5 2.2 %collective-permute-done.3.refs_3_ = bf16[128,2048]{1,0:T(8,128)(2,1)} collective-permute-done((bf16[128,2048]{1,0:T(8,128)(2,1)S(1)}, bf16[128,2048]{1,0:T(8,128)(2,1)}, u32[]{:S(2)}, u32[]{:S(2)}) %collective-permute-start.3) | collective-permute-done | bytes 524320 | tf_op jit(solution)/shard_map/ppermute | solution.py:37
  80.7 4.8 %project.1 = (f32[128,1024]{1,0:T(8,128)S(1)}, bf16[128,1024]{1,0:T(8,128)(2,1)S(1)}, bf16[128,1024]{1,0:T(8,128)(2,1)S(1)}, bf16[128,1024]{1,0:T(8,128)(2,1)S(1)}) custom-call(bf16[128,2048]{1,0:T(8,128)(2,1)S(1)} %get-tuple-element.23.refs_0_, bf16[128,2048]{1,0:T(8,128)(2,1)} %collective-permute-done.1.refs_1_, ...), custom_call_target="tpu_custom_call" | custom-call | flops 2147483648 | bytes 8388608 | tf_op jit(solution)/shard_map/project/pallas_call | solution.py:260
  85.5 0.7 copy-done.6
  86.2 0.7 copy-done.7
  86.9 1.1 reduce_sum.19
  88.0 0.8 broadcast_in_dim.7
  88.9 3.6 %all-to-all-start.2 = ((bf16[16,32,512]{2,1,0:T(8,128)(2,1)}), bf16[16,32,512]{2,1,0:T(8,128)(2,1)S(1)}, u32[]{:S(2)}, u32[]{:S(2)}) async-start(bf16[16,32,512]{2,1,0:T(8,128)(2,1)} %broadcast_in_dim.7), calls=%async_computation.2 | async-start | bytes 1048576 | tf_op jit(solution)/shard_map/all_to_all | solution.py:199
  92.4 4.9 %collective-permute-start.7 = (bf16[128,1024]{1,0:T(8,128)(2,1)}, bf16[128,1024]{1,0:T(8,128)(2,1)}, u32[]{:S(2)}, u32[]{:S(2)}) collective-permute-start(bf16[128,1024]{1,0:T(8,128)(2,1)} %copy-done.7), channel_id=1, source_target_pairs={{0,6},{2,0},{4,2},{6,4},{1,7},{3,1},{5,3},{7,5},{8,14},{10,8},{12,... | collective-permute-start | bytes 786440 | tf_op jit(solution)/shard_map/ppermute | solution.py:37
  97.4 3.2 %collective-permute-start.8 = (bf16[128,1024]{1,0:T(8,128)(2,1)}, bf16[128,1024]{1,0:T(8,128)(2,1)}, u32[]{:S(2)}, u32[]{:S(2)}) collective-permute-start(bf16[128,1024]{1,0:T(8,128)(2,1)} %copy-done.6), channel_id=1, source_target_pairs={{0,4},{2,6},{4,0},{6,2},{1,5},{3,7},{5,1},{7,3},{8,12},{10,14},{12... | collective-permute-start | bytes 786440 | tf_op jit(solution)/shard_map/ppermute | solution.py:37
  100.5 1.9 %collective-permute-start.9 = (bf16[128,1024]{1,0:T(8,128)(2,1)S(1)}, bf16[128,1024]{1,0:T(8,128)(2,1)}, u32[]{:S(2)}, u32[]{:S(2)}) collective-permute-start(bf16[128,1024]{1,0:T(8,128)(2,1)S(1)} %get-tuple-element.38), channel_id=1, source_target_pairs={{0,2},{2,4},{4,6},{6,0},{1,3},{3,5},{5,7},{7,1},{8,10},{10,12},{12... | collective-permute-start | bytes 786440 | tf_op jit(solution)/shard_map/ppermute | solution.py:37
  102.5 6.7 %all-to-all-done.2 = bf16[16,32,512]{2,1,0:T(8,128)(2,1)S(1)} async-done(((bf16[16,32,512]{2,1,0:T(8,128)(2,1)}), bf16[16,32,512]{2,1,0:T(8,128)(2,1)S(1)}, u32[]{:S(2)}, u32[]{:S(2)}) %all-to-all-start.2) | async-done | bytes 524320 | tf_op jit(solution)/shard_map/all_to_all | solution.py:199
  109.2 3.6 %collective-permute-start.6 = (bf16[512,512]{1,0:T(8,128)(2,1)S(1)}, bf16[512,512]{1,0:T(8,128)(2,1)S(1)}, u32[]{:S(2)}, u32[]{:S(2)}) collective-permute-start(bf16[512,512]{1,0:T(8,128)(2,1)S(1)} %bitcast.9), channel_id=1, source_target_pairs={{0,8},{8,0},{1,9},{9,1},{2,10},{10,2},{3,11},{11,3},{4,12},{12,4},... | collective-permute-start | bytes 1572872 | tf_op jit(solution)/shard_map/ppermute | solution.py:37
  112.8 2.1 %collective-permute-done.9 = bf16[128,1024]{1,0:T(8,128)(2,1)} collective-permute-done((bf16[128,1024]{1,0:T(8,128)(2,1)S(1)}, bf16[128,1024]{1,0:T(8,128)(2,1)}, u32[]{:S(2)}, u32[]{:S(2)}) %collective-permute-start.9) | collective-permute-done | bytes 262176 | tf_op jit(solution)/shard_map/ppermute | solution.py:37
  114.9 2.0 %add_convert_fusion.1 = bf16[128,1024]{1,0:T(8,128)(2,1)} fusion(bf16[128,1024]{1,0:T(8,128)(2,1)} %collective-permute-done.9, bf16[128,1024]{1,0:T(8,128)(2,1)} %collective-permute-done.8, f32[128,1024]{1,0:T(8,128)S(1)} %get-tuple-element.35, bf16[128,1024]{1,0:T(8,128)(2,1)} %collective-permute-done.7), kind=kLoop, calls=%fused_computation.2 | loop fusion | flops 917504 | bytes 1572864 | tf_op jit(solution)/shard_map/convert_element_type | solution.py:322
  116.9 3.0 %update.1 = (bf16[1024,512]{1,0:T(8,128)(2,1)}, f32[1024,512]{1,0:T(8,128)}) custom-call(s32[3]{0:T(128)S(1)} %pad_add_fusion.place, bf16[512,512]{1,0:T(8,128)(2,1)S(1)} %bitcast.10, bf16[512,512]{1,0:T(8,128)(2,1)S(1)} %collective-permute-done.6.other, bf16[1024,512]{1,0:T(8,128)(2,1)S(1)} %copy-done.1, f32[1024,512]{1,0:T(8,128)S(1)} %copy-done), custom_call_target="tpu_custom_call" | custom-call | flops 4194304 | bytes 7340032 | tf_op jit(solution)/shard_map/update/pallas_call | solution.py:172
  (22 shorter events, 0.1 us)
Async XLA Ops:
  1.5 1.2 %copy-start.2 = (bf16[1,1024,512]{2,1,0:T(8,128)(2,1)S(1)}, bf16[1,1024,512]{2,1,0:T(8,128)(2,1)}, u32[]{:S(2)}) copy-start(bf16[1,1024,512]{2,1,0:T(8,128)(2,1)} %param.7) | copy-start | bytes 3145732
  2.7 0.7 copy-start.3
  7.1 15.3 %copy-start.4 = (bf16[128,2048]{1,0:T(8,128)(2,1)}, bf16[128,2048]{1,0:T(8,128)(2,1)S(1)}, u32[]{:S(2)}) copy-start(bf16[128,2048]{1,0:T(8,128)(2,1)S(1)} %get-tuple-element.25) | copy-start | bytes 1572868
  7.1 15.3 %copy-start.5 = (bf16[128,2048]{1,0:T(8,128)(2,1)}, bf16[128,2048]{1,0:T(8,128)(2,1)S(1)}, u32[]{:S(2)}) copy-start(bf16[128,2048]{1,0:T(8,128)(2,1)S(1)} %get-tuple-element.24) | copy-start | bytes 1572868
  7.2 14.4 %collective-permute-start = (bf16[512,512]{1,0:T(8,128)(2,1)S(1)}, bf16[512,512]{1,0:T(8,128)(2,1)S(1)}, u32[]{:S(2)}, u32[]{:S(2)}) collective-permute-start(bf16[512,512]{1,0:T(8,128)(2,1)S(1)} %get-tuple-element.22), channel_id=1, source_target_pairs={{0,8},{8,0},{1,9},{9,1},{2,10},{10,2},{3,11},{11,3},{4,12},{12,4},... | collective-permute-start | bytes 1572872 | tf_op jit(solution)/shard_map/ppermute | solution.py:37
  19.6 26.4 %collective-permute-start.4 = (bf16[2,512,512]{2,1,0:T(8,128)(2,1)S(1)}, bf16[2,512,512]{2,1,0:T(8,128)(2,1)S(1)}, u32[]{:S(2)}, u32[]{:S(2)}) collective-permute-start(bf16[2,512,512]{2,1,0:T(8,128)(2,1)S(1)} %get-tuple-element.27), channel_id=1, source_target_pairs={{0,1},{8,585},{1,192},{9,8},{192,193},{200,9},{193,384},{201,200},... | collective-permute-start | bytes 3145736 | tf_op jit(solution)/shard_map/ppermute | solution.py:293
  22.5 36.3 %all-to-all-start = ((bf16[16,32,512]{2,1,0:T(8,128)(2,1)}), bf16[16,32,512]{2,1,0:T(8,128)(2,1)}, u32[]{:S(2)}, u32[]{:S(2)}) async-start(bf16[16,32,512]{2,1,0:T(8,128)(2,1)} %bitcast.13), calls=%async_computation | async-start | bytes 1048576 | tf_op jit(solution)/shard_map/all_to_all | solution.py:208
  45.9 34.8 %collective-permute-start.5 = (bf16[2,512,512]{2,1,0:T(8,128)(2,1)S(1)}, bf16[2,512,512]{2,1,0:T(8,128)(2,1)S(1)}, u32[]{:S(2)}, u32[]{:S(2)}) collective-permute-start(bf16[2,512,512]{2,1,0:T(8,128)(2,1)S(1)} %collective-permute-done.4.refs_5_), channel_id=1, source_target_pairs={{0,8},{8,0},{1,9},{9,1},{2,10},{10,2},{3,11},{11,3},{4,12},{12,4},... | collective-permute-start | bytes 3145736 | tf_op jit(solution)/shard_map/ppermute | solution.py:37
  50.3 28.2 %collective-permute-start.1 = (bf16[128,2048]{1,0:T(8,128)(2,1)}, bf16[128,2048]{1,0:T(8,128)(2,1)}, u32[]{:S(2)}, u32[]{:S(2)}) collective-permute-start(bf16[128,2048]{1,0:T(8,128)(2,1)} %copy-done.5), channel_id=1, source_target_pairs={{0,2},{2,4},{4,6},{6,0},{1,3},{3,5},{5,7},{7,1},{8,10},{10,12},{12... | collective-permute-start | bytes 1572872 | tf_op jit(solution)/shard_map/ppermute | solution.py:37
  52.2 26.3 %collective-permute-start.2 = (bf16[128,2048]{1,0:T(8,128)(2,1)}, bf16[128,2048]{1,0:T(8,128)(2,1)}, u32[]{:S(2)}, u32[]{:S(2)}) collective-permute-start(bf16[128,2048]{1,0:T(8,128)(2,1)} %copy-done.4), channel_id=1, source_target_pairs={{0,4},{2,6},{4,0},{6,2},{1,5},{3,7},{5,1},{7,3},{8,12},{10,14},{12... | collective-permute-start | bytes 1572872 | tf_op jit(solution)/shard_map/ppermute | solution.py:37
  54.1 26.6 %collective-permute-start.3 = (bf16[128,2048]{1,0:T(8,128)(2,1)S(1)}, bf16[128,2048]{1,0:T(8,128)(2,1)}, u32[]{:S(2)}, u32[]{:S(2)}) collective-permute-start(bf16[128,2048]{1,0:T(8,128)(2,1)S(1)} %get-tuple-element.26), channel_id=1, source_target_pairs={{0,6},{2,0},{4,2},{6,4},{1,7},{3,1},{5,3},{7,5},{8,14},{10,8},{12,... | collective-permute-start | bytes 1572872 | tf_op jit(solution)/shard_map/ppermute | solution.py:37
  60.6 26.3 %all-to-all-start.1 = ((f32[3,32,512]{2,1,0:T(8,128)}), f32[3,32,512]{2,1,0:T(8,128)}, u32[]{:S(2)}, u32[]{:S(2)}) async-start(f32[3,32,512]{2,1,0:T(8,128)} %broadcast_in_dim.6), calls=%async_computation.1 | async-start | bytes 393216 | tf_op jit(solution)/shard_map/all_to_all | solution.py:214
  85.5 0.7 copy-start.6
  86.2 0.7 copy-start.7
  86.9 30.0 %copy-start = (f32[1024,512]{1,0:T(8,128)S(1)}, f32[1024,512]{1,0:T(8,128)}, u32[]{:S(2)}) copy-start(f32[1024,512]{1,0:T(8,128)} %momentum.1) | copy-start | bytes 6291460
  88.9 20.3 %all-to-all-start.2 = ((bf16[16,32,512]{2,1,0:T(8,128)(2,1)}), bf16[16,32,512]{2,1,0:T(8,128)(2,1)S(1)}, u32[]{:S(2)}, u32[]{:S(2)}) async-start(bf16[16,32,512]{2,1,0:T(8,128)(2,1)} %broadcast_in_dim.7), calls=%async_computation.2 | async-start | bytes 1048576 | tf_op jit(solution)/shard_map/all_to_all | solution.py:199
  92.4 20.4 %collective-permute-start.7 = (bf16[128,1024]{1,0:T(8,128)(2,1)}, bf16[128,1024]{1,0:T(8,128)(2,1)}, u32[]{:S(2)}, u32[]{:S(2)}) collective-permute-start(bf16[128,1024]{1,0:T(8,128)(2,1)} %copy-done.7), channel_id=1, source_target_pairs={{0,6},{2,0},{4,2},{6,4},{1,7},{3,1},{5,3},{7,5},{8,14},{10,8},{12,... | collective-permute-start | bytes 786440 | tf_op jit(solution)/shard_map/ppermute | solution.py:37
  97.4 15.5 %collective-permute-start.8 = (bf16[128,1024]{1,0:T(8,128)(2,1)}, bf16[128,1024]{1,0:T(8,128)(2,1)}, u32[]{:S(2)}, u32[]{:S(2)}) collective-permute-start(bf16[128,1024]{1,0:T(8,128)(2,1)} %copy-done.6), channel_id=1, source_target_pairs={{0,4},{2,6},{4,0},{6,2},{1,5},{3,7},{5,1},{7,3},{8,12},{10,14},{12... | collective-permute-start | bytes 786440 | tf_op jit(solution)/shard_map/ppermute | solution.py:37
  100.5 14.4 %collective-permute-start.9 = (bf16[128,1024]{1,0:T(8,128)(2,1)S(1)}, bf16[128,1024]{1,0:T(8,128)(2,1)}, u32[]{:S(2)}, u32[]{:S(2)}) collective-permute-start(bf16[128,1024]{1,0:T(8,128)(2,1)S(1)} %get-tuple-element.38), channel_id=1, source_target_pairs={{0,2},{2,4},{4,6},{6,0},{1,3},{3,5},{5,7},{7,1},{8,10},{10,12},{12... | collective-permute-start | bytes 786440 | tf_op jit(solution)/shard_map/ppermute | solution.py:37
  109.2 7.7 %copy-start.1 = (bf16[1024,512]{1,0:T(8,128)(2,1)S(1)}, bf16[1024,512]{1,0:T(8,128)(2,1)}, u32[]{:S(2)}) copy-start(bf16[1024,512]{1,0:T(8,128)(2,1)} %base.1) | copy-start | bytes 3145732
  109.2 7.7 %collective-permute-start.6 = (bf16[512,512]{1,0:T(8,128)(2,1)S(1)}, bf16[512,512]{1,0:T(8,128)(2,1)S(1)}, u32[]{:S(2)}, u32[]{:S(2)}) collective-permute-start(bf16[512,512]{1,0:T(8,128)(2,1)S(1)} %bitcast.9), channel_id=1, source_target_pairs={{0,8},{8,0},{1,9},{9,1},{2,10},{10,2},{3,11},{11,3},{4,12},{12,4},... | collective-permute-start | bytes 1572872 | tf_op jit(solution)/shard_map/ppermute | solution.py:37

commit v3 on v2

--- a/solution.py
+++ b/solution.py
@@ -41,12 +41,12 @@
     return pl.BlockSpec(memory_space=pl.ANY)
 
 
-def front_kernel(place, gain, exponents, tokens, values, weight, *refs):
-    (*blocks, keep, send, share), scratch = refs[: -len(FRONT)], refs[-len(FRONT) :]
+def front_kernel(place, gain, exponents, tokens, values, *refs):
+    (*blocks, keep, send), scratch = refs[: -len(FRONT)], refs[-len(FRONT) :]
     x, yl, core = place[0], place[1], place[2]
-    held, normed, delta, dequantized, token_in, block_out, delta_in, delta_out, moved = scratch
+    held, normed, delta, dequantized, token_in, block_out, delta_in, delta_out = scratch
     peers, rows, block = normed.shape
-    half, quarter = block // 2, block // 4
+    half = block // 2
 
     def chunk(i):
         at = pl.ds(i * block, block)
@@ -56,10 +56,6 @@
         chunk(i).start()
     delta_copy = pltpu.make_async_copy(values, delta, delta_in)
     delta_copy.start()
-    depth = share.shape[1]
-    mine = pl.ds(pl.multiple_of(core * depth, depth), depth)
-    share_copy = pltpu.make_async_copy(weight.at[:, mine, :], share, moved)
-    share_copy.start()
 
     total = jnp.zeros((rows, 128), f32)
     for i in range(peers):
@@ -72,14 +68,10 @@
     outs = []
     for k in (*range(1, peers), 0):
         first = lax.rem(x + k, peers) * block
-        for at, start, size in (
-            (0, yl * half, half),
-            (half, (1 - yl) * half + core * quarter, quarter),
-            (half + quarter, (1 - yl) * half + (1 - core) * quarter, quarter),
-        ):
-            columns = pl.ds(pl.multiple_of(first + start, quarter), size)
+        for at, part in ((0, yl), (half, 1 - yl)):
+            columns = pl.ds(pl.multiple_of(first + part * half, half), half)
             piece = held[:, columns].astype(f32) * scale * gain[:, columns].astype(f32)
-            normed[k, :, at : at + size] = piece.astype(bf16)
+            normed[k, :, at : at + half] = piece.astype(bf16)
         outs.append(pltpu.make_async_copy(normed.at[k], blocks[k], block_out.at[k]))
         outs[-1].start()
 
@@ -97,27 +89,25 @@
         dequantized[i] = (delta[pl.ds(start, near), :].astype(f32) * wide).astype(bf16)
         outs.append(pltpu.make_async_copy(dequantized.at[i], out, delta_out.at[i]))
         outs[-1].start()
-    for copy in (*outs, share_copy):
+    for copy in outs:
         copy.wait()
 
 
-FRONT = ("held", "normed", "delta", "dequantized", "in", "out", "din", "dout", "moved")
-
-
-def front(place, tokens, gain, values, exponents, weight):
+FRONT = ("held", "normed", "delta", "dequantized", "in", "out", "din", "dout")
+
+
+def front(place, tokens, gain, values, exponents):
     rows, width = tokens.shape
     peers = lax.axis_size("x")
     block = width // peers
     deep, across = values.shape
-    kinds, depth, columns = weight.shape
     dma = pltpu.SemaphoreType.DMA
     return pl.pallas_call(
         front_kernel,
         out_shape=(jax.ShapeDtypeStruct((rows, block), bf16),) * peers
-        + (jax.ShapeDtypeStruct((deep // 2, across), bf16),) * 2
-        + (jax.ShapeDtypeStruct((kinds, depth // 2, columns), bf16),),
-        in_specs=[smem(), vmem(), vmem(), hbm(), hbm(), hbm()],
-        out_specs=(hbm(),) * (peers + 3),
+        + (jax.ShapeDtypeStruct((deep // 2, across), bf16),) * 2,
+        in_specs=[smem(), vmem(), vmem(), hbm(), hbm()],
+        out_specs=(hbm(),) * (peers + 2),
         scratch_shapes=[
             pltpu.VMEM((rows, width), bf16),
             pltpu.VMEM((peers, rows, block), bf16),
@@ -127,7 +117,6 @@
             dma((peers,)),
             dma,
             dma((2,)),
-            dma,
         ],
         compiler_params=params(),
         cost_estimate=pl.CostEstimate(
@@ -136,7 +125,7 @@
             transcendentals=0,
         ),
         name="front",
-    )(place, gain, exponents, tokens, values, weight)
+    )(place, gain, exponents, tokens, values)
 
 
 def update_kernel(place, own, other, base, momentum, new_params, new_momentum):
@@ -218,17 +207,14 @@
 
 
 def project_kernel(*refs):
-    ins, outs, scratch = refs[:7], refs[7:-7], refs[-7:]
-    *blocks, mine, near, far = ins
+    ins, outs, scratch = refs[:6], refs[6:-7], refs[-7:]
+    *blocks, mine, other = ins
     held, whole, first, rest, block_in, weight_in, out_sem = scratch
-    half, quarter, width = mine.shape[1], near.shape[1], mine.shape[2]
+    half, width = mine.shape[1], mine.shape[2]
     copies = []
-    for i, (part, at, size) in enumerate(
-        ((mine, 0, half), (near, half, quarter), (far, half + quarter, quarter))
-    ):
-        copies.append(
-            pltpu.make_async_copy(part, whole.at[:, at : at + size, :], weight_in.at[i])
-        )
+    for i, part in enumerate((mine, other)):
+        rows = whole.at[:, i * half : (i + 1) * half, :]
+        copies.append(pltpu.make_async_copy(part, rows, weight_in.at[i]))
     order = (*range(1, len(blocks)), 0)
     arrivals = {
         k: pltpu.make_async_copy(blocks[k], held.at[k], block_in.at[k]) for k in order
@@ -261,7 +247,7 @@
         project_kernel,
         out_shape=(jax.ShapeDtypeStruct((rows, width), f32),)
         + (jax.ShapeDtypeStruct((rows, width), bf16),) * (n - 1),
-        in_specs=[hbm()] * (n + 3),
+        in_specs=[hbm()] * (n + 2),
         out_specs=(hbm(),) * n,
         scratch_shapes=[
             pltpu.VMEM((n, rows, depth), bf16),
@@ -269,7 +255,7 @@
             pltpu.VMEM((rows, width), f32),
             pltpu.VMEM((n - 1, rows, width), bf16),
             dma((n,)),
-            dma((3,)),
+            dma((2,)),
             dma((n,)),
         ],
         compiler_params=params(),
@@ -282,7 +268,7 @@
     )(*tokens, *weights)
 
 
-def neighbour_share(share):
+def neighbour_weights(weight):
     yh, cores, yl = (lax.axis_size(a) for a in ("yh", "core", "yl"))
     ys = yh * yl
     moves = []
@@ -290,7 +276,7 @@
         for core in range(cores):
             to = (y + (1 if core == 0 else -1)) % ys
             moves.append(tuple((v // yl * cores + core) * yl + v % yl for v in (y, to)))
-    return lax.ppermute(share, ("yh", "core", "yl"), moves)
+    return lax.ppermute(weight, ("yh", "core", "yl"), moves)
 
 
 def body(pseudo_grad, block_exponent, base_params, outer_momentum, tokens, norm_gain, kv_weight):
@@ -298,19 +284,18 @@
     place = jnp.stack([x, yl, core]).astype(jnp.int32)
     after = lax.optimization_barrier
 
-    *blocks, keep, send, share = front(
-        place, tokens, norm_gain.reshape(1, -1), pseudo_grad[0], block_exponent[0].T, kv_weight
+    *blocks, keep, send = front(
+        place, tokens, norm_gain.reshape(1, -1), pseudo_grad[0], block_exponent[0].T
     )
     arrived = [blocks[0]] + [shift(block, "x", k) for k, block in enumerate(blocks) if k]
-    near = neighbour_share(share)
+    near = neighbour_weights(kv_weight)
     got = shift(send, "core", 1)
 
     pair = (keep.astype(f32) + got.astype(f32)).astype(bf16)
     total = scatter_group(pair)
-    far = shift(near, "core", 1)
     average = (sum_thirds(total) / lax.axis_size(REPLICA)).astype(bf16)
 
-    partial = project(arrived, (kv_weight, near, far))
+    partial = project(arrived, (kv_weight, near))
     average, *partial = after((average, *partial))
     average = gather_group(average)
     other = shift(average, "core", 1)

time: 121 us -> 115 us (0.950)
  waiting for transfers between devices: 42.5 us -> 25.8 us
  starting transfers between devices: 54.2 us -> 64.4 us
    ppermute x1, waiting for transfers between devices: 19.2 us -> 0.01 us  [neighbour_weights(): return lax.ppermute(weight, ('yh', 'core', 'yl'), moves)]
    all_to_all x1, waiting for transfers between devices: 0.01 us -> 18.5 us  [scatter_group(): parts = lax.all_to_all(parts, GROUP, 0, 0, tiled=True)]
    ppermute x9 -> x8, waiting for transfers between devices: 16.6 us -> 0.02 us  [shift(): return lax.ppermute(value, axis, [(i, (i + by) % n) for i in range(n)])]
    all_to_all x1, starting transfers between devices: 3.57 us -> 13.2 us  [gather_group(): lax.all_to_all(jnp.broadcast_to(value, (group, *value.shape)), GROUP, 0,...]
    all_to_all x1, starting transfers between devices: 5.67 us -> 8.54 us  [sum_thirds(): lax.all_to_all(jnp.broadcast_to(value, (third, *value.shape)), 'zh', 0, 0...]
    ppermute x9 -> x8, starting transfers between devices: 38.8 us -> 36.5 us  [shift(): return lax.ppermute(value, axis, [(i, (i + by) % n) for i in range(n)])]
    unnamed x16 -> x18, local copies, waits for them, and re-layouts: 3.36 us -> 3.36 us
  transfers between devices with their start and end apart: 13 -> 12, of which waited for: 5 -> 3; matrix products, arithmetic and copies ran while one was open for 4% -> 4% of each run, Pallas kernels for 4% -> 5%
where the time goes in v3:
time: 115 us; the launch traced here: 114 us
  starting transfers between devices  64.4 us (56%)
  waiting for transfers between devices  25.8 us (22%)
  Pallas kernels  12 us (10%)
  local copies, waits for them, and re-layouts  5.64 us (5%)
  other arithmetic  5.07 us (4%)
    ppermute x8, starting transfers between devices, shift(): return lax.ppermute(value, axis, [(i, (i + by) % n) for i in range(n)])  36.5 us
    all_to_all x1, waiting for transfers between devices, scatter_group(): parts = lax.all_to_all(parts, GROUP, 0, 0, tiled=True)  18.5 us
    all_to_all x1, starting transfers between devices, gather_group(): lax.all_to_all(jnp.broadcast_to(value, (group, *value.shape)), GROUP, 0,...  13.2 us
    all_to_all x1, starting transfers between devices, sum_thirds(): lax.all_to_all(jnp.broadcast_to(value, (third, *value.shape)), 'zh', 0, 0...  8.54 us
    all_to_all x1, waiting for transfers between devices, gather_group(): lax.all_to_all(jnp.broadcast_to(value, (group, *value.shape)), GROUP, 0,...  6.19 us
    pallas_call x1, Pallas kernels, project(): pl.pallas_call(project_kernel, out_shape=(jax.ShapeDtypeStruct((rows, wid...  5.15 us
    all_to_all x1, starting transfers between devices, scatter_group(): parts = lax.all_to_all(parts, GROUP, 0, 0, tiled=True)  4.24 us
    pallas_call x1, Pallas kernels, front(): pl.pallas_call(front_kernel, out_shape=(jax.ShapeDtypeStruct((rows, block...  3.81 us
  transfers between devices with their start and end apart: 12, of which 3 were waited for; matrix products, arithmetic and copies ran while one was open for 4% of the time, Pallas kernels for 5%

profile of v3, /device:TPU:1, one launch (start us, length us, event | category | flops | bytes accessed | tf_op | source)
XLA Modules:
  0.0 113.7 jit_solution(7971924156543931670)
XLA Ops:
  0.6 0.7 reshape.15.gain
  1.4 0.1 pad_add_fusion.place
  1.5 1.2 %copy-done.2 = bf16[1,1024,512]{2,1,0:T(8,128)(2,1)S(1)} copy-done((bf16[1,1024,512]{2,1,0:T(8,128)(2,1)S(1)}, bf16[1,1024,512]{2,1,0:T(8,128)(2,1)}, u32[]{:S(2)}) %copy-start.2) | copy-done | bytes 1048600
  2.7 0.7 copy-done.3
  3.4 3.8 %front.1 = (bf16[128,2048]{1,0:T(8,128)(2,1)S(1)}, bf16[128,2048]{1,0:T(8,128)(2,1)S(1)}, bf16[128,2048]{1,0:T(8,128)(2,1)S(1)}, bf16[128,2048]{1,0:T(8,128)(2,1...) custom-call(s32[3]{0:T(128)S(1)} %pad_add_fusion.place, bf16[1,8192]{1,0:T(2,128)(2,1)S(1)} %reshape.15.gain, ...), custom_call_target="tpu_custom_call" | custom-call | flops 8388608 | bytes 6291456 | tf_op jit(solution)/shard_map/front/pallas_call | solution.py:105
  7.2 0.0 copy-start.6
  7.2 12.4 %collective-permute-start = (bf16[512,512]{1,0:T(8,128)(2,1)S(1)}, bf16[512,512]{1,0:T(8,128)(2,1)S(1)}, u32[]{:S(2)}, u32[]{:S(2)}) collective-permute-start(bf16[512,512]{1,0:T(8,128)(2,1)S(1)} %get-tuple-element.21), channel_id=1, source_target_pairs={{0,8},{8,0},{1,9},{9,1},{2,10},{10,2},{3,11},{11,3},{4,12},{12,4},... | collective-permute-start | bytes 1572872 | tf_op jit(solution)/shard_map/ppermute | solution.py:37
  19.7 1.9 %collective-permute-start.4 = (bf16[2,1024,512]{2,1,0:T(8,128)(2,1)S(1)}, bf16[2,1024,512]{2,1,0:T(8,128)(2,1)}, u32[]{:S(2)}, u32[]{:S(2)}) collective-permute-start(bf16[2,1024,512]{2,1,0:T(8,128)(2,1)S(1)} %copy-done.4), channel_id=1, source_target_pairs={{0,1},{8,585},{1,192},{9,8},{192,193},{200,9},{193,384},{201,200},... | collective-permute-start | bytes 6291464 | tf_op jit(solution)/shard_map/ppermute | solution.py:279
  21.6 0.9 add_convert_fusion
  22.6 4.2 %all-to-all-start = ((bf16[16,32,512]{2,1,0:T(8,128)(2,1)}), bf16[16,32,512]{2,1,0:T(8,128)(2,1)}, u32[]{:S(2)}, u32[]{:S(2)}) async-start(bf16[16,32,512]{2,1,0:T(8,128)(2,1)} %bitcast.13), calls=%async_computation | async-start | bytes 1048576 | tf_op jit(solution)/shard_map/all_to_all | solution.py:197
  26.8 2.4 %collective-permute-start.1 = (bf16[128,2048]{1,0:T(8,128)(2,1)}, bf16[128,2048]{1,0:T(8,128)(2,1)}, u32[]{:S(2)}, u32[]{:S(2)}) collective-permute-start(bf16[128,2048]{1,0:T(8,128)(2,1)} %copy-done.6), channel_id=1, source_target_pairs={{0,2},{2,4},{4,6},{6,0},{1,3},{3,5},{5,7},{7,1},{8,10},{10,12},{12... | collective-permute-start | bytes 1572872 | tf_op jit(solution)/shard_map/ppermute | solution.py:37
  29.3 4.4 %collective-permute-start.2 = (bf16[128,2048]{1,0:T(8,128)(2,1)}, bf16[128,2048]{1,0:T(8,128)(2,1)}, u32[]{:S(2)}, u32[]{:S(2)}) collective-permute-start(bf16[128,2048]{1,0:T(8,128)(2,1)} %copy-done.5), channel_id=1, source_target_pairs={{0,4},{2,6},{4,0},{6,2},{1,5},{3,7},{5,1},{7,3},{8,12},{10,14},{12... | collective-permute-start | bytes 1572872 | tf_op jit(solution)/shard_map/ppermute | solution.py:37
  33.6 3.1 %collective-permute-start.3 = (bf16[128,2048]{1,0:T(8,128)(2,1)S(1)}, bf16[128,2048]{1,0:T(8,128)(2,1)}, u32[]{:S(2)}, u32[]{:S(2)}) collective-permute-start(bf16[128,2048]{1,0:T(8,128)(2,1)S(1)} %get-tuple-element.25), channel_id=1, source_target_pairs={{0,6},{2,0},{4,2},{6,4},{1,7},{3,1},{5,3},{7,5},{8,14},{10,8},{12,... | collective-permute-start | bytes 1572872 | tf_op jit(solution)/shard_map/ppermute | solution.py:37
  36.7 18.5 %all-to-all-done = bf16[16,32,512]{2,1,0:T(8,128)(2,1)} async-done(((bf16[16,32,512]{2,1,0:T(8,128)(2,1)}), bf16[16,32,512]{2,1,0:T(8,128)(2,1)}, u32[]{:S(2)}, u32[]{:S(2)}) %all-to-all-start) | async-done | bytes 524320 | tf_op jit(solution)/shard_map/all_to_all | solution.py:197
  55.2 1.1 convert_reduce_fusion
  56.3 0.7 broadcast_in_dim.6
  57.0 8.5 %all-to-all-start.1 = ((f32[3,32,512]{2,1,0:T(8,128)}), f32[3,32,512]{2,1,0:T(8,128)}, u32[]{:S(2)}, u32[]{:S(2)}) async-start(f32[3,32,512]{2,1,0:T(8,128)} %broadcast_in_dim.6), calls=%async_computation.1 | async-start | bytes 393216 | tf_op jit(solution)/shard_map/all_to_all | solution.py:203
  65.6 5.1 %project.1 = (f32[128,1024]{1,0:T(8,128)S(1)}, bf16[128,1024]{1,0:T(8,128)(2,1)S(1)}, bf16[128,1024]{1,0:T(8,128)(2,1)S(1)}, bf16[128,1024]{1,0:T(8,128)(2,1)S(1)}) custom-call(bf16[128,2048]{1,0:T(8,128)(2,1)S(1)} %get-tuple-element.22.refs_0_, bf16[128,2048]{1,0:T(8,128)(2,1)} %collective-permute-done.1.refs_1_, ...), custom_call_target="tpu_custom_call" | custom-call | flops 2147483648 | bytes 8388608 | tf_op jit(solution)/shard_map/project/pallas_call | solution.py:246
  70.8 0.0 copy-start.7
  70.8 0.7 copy-done.7
  71.5 0.7 copy-done.8
  72.2 1.0 all-to-all-done.1
  73.2 0.9 reduce_sum.19
  74.2 0.8 broadcast_in_dim.7
  75.0 13.2 %all-to-all-start.2 = ((bf16[16,32,512]{2,1,0:T(8,128)(2,1)}), bf16[16,32,512]{2,1,0:T(8,128)(2,1)S(1)}, u32[]{:S(2)}, u32[]{:S(2)}) async-start(bf16[16,32,512]{2,1,0:T(8,128)(2,1)} %broadcast_in_dim.7), calls=%async_computation.2 | async-start | bytes 1048576 | tf_op jit(solution)/shard_map/all_to_all | solution.py:188
  88.2 3.1 %collective-permute-start.8 = (bf16[128,1024]{1,0:T(8,128)(2,1)}, bf16[128,1024]{1,0:T(8,128)(2,1)}, u32[]{:S(2)}, u32[]{:S(2)}) collective-permute-start(bf16[128,1024]{1,0:T(8,128)(2,1)} %copy-done.8), channel_id=1, source_target_pairs={{0,2},{2,4},{4,6},{6,0},{1,3},{3,5},{5,7},{7,1},{8,10},{10,12},{12... | collective-permute-start | bytes 786440 | tf_op jit(solution)/shard_map/ppermute | solution.py:37
  91.3 4.4 %collective-permute-start.7 = (bf16[128,1024]{1,0:T(8,128)(2,1)}, bf16[128,1024]{1,0:T(8,128)(2,1)}, u32[]{:S(2)}, u32[]{:S(2)}) collective-permute-start(bf16[128,1024]{1,0:T(8,128)(2,1)} %copy-done.7), channel_id=1, source_target_pairs={{0,4},{2,6},{4,0},{6,2},{1,5},{3,7},{5,1},{7,3},{8,12},{10,14},{12... | collective-permute-start | bytes 786440 | tf_op jit(solution)/shard_map/ppermute | solution.py:37
  95.7 3.1 %collective-permute-start.6 = (bf16[128,1024]{1,0:T(8,128)(2,1)S(1)}, bf16[128,1024]{1,0:T(8,128)(2,1)}, u32[]{:S(2)}, u32[]{:S(2)}) collective-permute-start(bf16[128,1024]{1,0:T(8,128)(2,1)S(1)} %get-tuple-element.34), channel_id=1, source_target_pairs={{0,6},{2,0},{4,2},{6,4},{1,7},{3,1},{5,3},{7,5},{8,14},{10,8},{12,... | collective-permute-start | bytes 786440 | tf_op jit(solution)/shard_map/ppermute | solution.py:37
  98.8 6.2 %all-to-all-done.2 = bf16[16,32,512]{2,1,0:T(8,128)(2,1)S(1)} async-done(((bf16[16,32,512]{2,1,0:T(8,128)(2,1)}), bf16[16,32,512]{2,1,0:T(8,128)(2,1)S(1)}, u32[]{:S(2)}, u32[]{:S(2)}) %all-to-all-start.2) | async-done | bytes 524320 | tf_op jit(solution)/shard_map/all_to_all | solution.py:188
  104.9 3.7 %collective-permute-start.5 = (bf16[512,512]{1,0:T(8,128)(2,1)S(1)}, bf16[512,512]{1,0:T(8,128)(2,1)S(1)}, u32[]{:S(2)}, u32[]{:S(2)}) collective-permute-start(bf16[512,512]{1,0:T(8,128)(2,1)S(1)} %bitcast.9), channel_id=1, source_target_pairs={{0,8},{8,0},{1,9},{9,1},{2,10},{10,2},{3,11},{11,3},{4,12},{12,4},... | collective-permute-start | bytes 1572872 | tf_op jit(solution)/shard_map/ppermute | solution.py:37
  108.7 2.0 %add_convert_fusion.1 = bf16[128,1024]{1,0:T(8,128)(2,1)} fusion(bf16[128,1024]{1,0:T(8,128)(2,1)} %collective-permute-done.8, bf16[128,1024]{1,0:T(8,128)(2,1)} %collective-permute-done.7, f32[128,1024]{1,0:T(8,128)S(1)} %get-tuple-element.33, bf16[128,1024]{1,0:T(8,128)(2,1)} %collective-permute-done.6), kind=kLoop, calls=%fused_computation.2 | loop fusion | flops 917504 | bytes 1572864 | tf_op jit(solution)/shard_map/convert_element_type | solution.py:307
  110.7 3.0 %update.1 = (bf16[1024,512]{1,0:T(8,128)(2,1)}, f32[1024,512]{1,0:T(8,128)}) custom-call(s32[3]{0:T(128)S(1)} %pad_add_fusion.place, bf16[512,512]{1,0:T(8,128)(2,1)S(1)} %bitcast.10, bf16[512,512]{1,0:T(8,128)(2,1)S(1)} %collective-permute-done.5.other, bf16[1024,512]{1,0:T(8,128)(2,1)S(1)} %copy-done.1, f32[1024,512]{1,0:T(8,128)S(1)} %copy-done), custom_call_target="tpu_custom_call" | custom-call | flops 4194304 | bytes 7340032 | tf_op jit(solution)/shard_map/update/pallas_call | solution.py:161
  (22 shorter events, 0.1 us)
Async XLA Ops:
  1.5 1.2 %copy-start.2 = (bf16[1,1024,512]{2,1,0:T(8,128)(2,1)S(1)}, bf16[1,1024,512]{2,1,0:T(8,128)(2,1)}, u32[]{:S(2)}) copy-start(bf16[1,1024,512]{2,1,0:T(8,128)(2,1)} %param.7) | copy-start | bytes 3145732
  2.7 0.7 copy-start.3
  3.4 16.3 %copy-start.4 = (bf16[2,1024,512]{2,1,0:T(8,128)(2,1)S(1)}, bf16[2,1024,512]{2,1,0:T(8,128)(2,1)}, u32[]{:S(2)}) copy-start(bf16[2,1024,512]{2,1,0:T(8,128)(2,1)} %refs_4_.1) | copy-start | bytes 6291460
  7.2 15.3 %copy-start.5 = (bf16[128,2048]{1,0:T(8,128)(2,1)}, bf16[128,2048]{1,0:T(8,128)(2,1)S(1)}, u32[]{:S(2)}) copy-start(bf16[128,2048]{1,0:T(8,128)(2,1)S(1)} %get-tuple-element.24) | copy-start | bytes 1572868
  7.2 15.3 %copy-start.6 = (bf16[128,2048]{1,0:T(8,128)(2,1)}, bf16[128,2048]{1,0:T(8,128)(2,1)S(1)}, u32[]{:S(2)}) copy-start(bf16[128,2048]{1,0:T(8,128)(2,1)S(1)} %get-tuple-element.23) | copy-start | bytes 1572868
  7.2 14.4 %collective-permute-start = (bf16[512,512]{1,0:T(8,128)(2,1)S(1)}, bf16[512,512]{1,0:T(8,128)(2,1)S(1)}, u32[]{:S(2)}, u32[]{:S(2)}) collective-permute-start(bf16[512,512]{1,0:T(8,128)(2,1)S(1)} %get-tuple-element.21), channel_id=1, source_target_pairs={{0,8},{8,0},{1,9},{9,1},{2,10},{10,2},{3,11},{11,3},{4,12},{12,4},... | collective-permute-start | bytes 1572872 | tf_op jit(solution)/shard_map/ppermute | solution.py:37
  19.7 45.9 %collective-permute-start.4 = (bf16[2,1024,512]{2,1,0:T(8,128)(2,1)S(1)}, bf16[2,1024,512]{2,1,0:T(8,128)(2,1)}, u32[]{:S(2)}, u32[]{:S(2)}) collective-permute-start(bf16[2,1024,512]{2,1,0:T(8,128)(2,1)S(1)} %copy-done.4), channel_id=1, source_target_pairs={{0,1},{8,585},{1,192},{9,8},{192,193},{200,9},{193,384},{201,200},... | collective-permute-start | bytes 6291464 | tf_op jit(solution)/shard_map/ppermute | solution.py:279
  22.6 32.6 %all-to-all-start = ((bf16[16,32,512]{2,1,0:T(8,128)(2,1)}), bf16[16,32,512]{2,1,0:T(8,128)(2,1)}, u32[]{:S(2)}, u32[]{:S(2)}) async-start(bf16[16,32,512]{2,1,0:T(8,128)(2,1)} %bitcast.13), calls=%async_computation | async-start | bytes 1048576 | tf_op jit(solution)/shard_map/all_to_all | solution.py:197
  26.8 38.8 %collective-permute-start.1 = (bf16[128,2048]{1,0:T(8,128)(2,1)}, bf16[128,2048]{1,0:T(8,128)(2,1)}, u32[]{:S(2)}, u32[]{:S(2)}) collective-permute-start(bf16[128,2048]{1,0:T(8,128)(2,1)} %copy-done.6), channel_id=1, source_target_pairs={{0,2},{2,4},{4,6},{6,0},{1,3},{3,5},{5,7},{7,1},{8,10},{10,12},{12... | collective-permute-start | bytes 1572872 | tf_op jit(solution)/shard_map/ppermute | solution.py:37
  29.3 36.3 %collective-permute-start.2 = (bf16[128,2048]{1,0:T(8,128)(2,1)}, bf16[128,2048]{1,0:T(8,128)(2,1)}, u32[]{:S(2)}, u32[]{:S(2)}) collective-permute-start(bf16[128,2048]{1,0:T(8,128)(2,1)} %copy-done.5), channel_id=1, source_target_pairs={{0,4},{2,6},{4,0},{6,2},{1,5},{3,7},{5,1},{7,3},{8,12},{10,14},{12... | collective-permute-start | bytes 1572872 | tf_op jit(solution)/shard_map/ppermute | solution.py:37
  33.6 32.0 %collective-permute-start.3 = (bf16[128,2048]{1,0:T(8,128)(2,1)S(1)}, bf16[128,2048]{1,0:T(8,128)(2,1)}, u32[]{:S(2)}, u32[]{:S(2)}) collective-permute-start(bf16[128,2048]{1,0:T(8,128)(2,1)S(1)} %get-tuple-element.25), channel_id=1, source_target_pairs={{0,6},{2,0},{4,2},{6,4},{1,7},{3,1},{5,3},{7,5},{8,14},{10,8},{12,... | collective-permute-start | bytes 1572872 | tf_op jit(solution)/shard_map/ppermute | solution.py:37
  57.0 16.2 %all-to-all-start.1 = ((f32[3,32,512]{2,1,0:T(8,128)}), f32[3,32,512]{2,1,0:T(8,128)}, u32[]{:S(2)}, u32[]{:S(2)}) async-start(f32[3,32,512]{2,1,0:T(8,128)} %broadcast_in_dim.6), calls=%async_computation.1 | async-start | bytes 393216 | tf_op jit(solution)/shard_map/all_to_all | solution.py:203
  70.8 0.7 copy-start.7
  71.5 0.7 copy-start.8
  72.2 38.5 %copy-start = (f32[1024,512]{1,0:T(8,128)S(1)}, f32[1024,512]{1,0:T(8,128)}, u32[]{:S(2)}) copy-start(f32[1024,512]{1,0:T(8,128)} %momentum.1) | copy-start | bytes 6291460
  75.0 29.9 %all-to-all-start.2 = ((bf16[16,32,512]{2,1,0:T(8,128)(2,1)}), bf16[16,32,512]{2,1,0:T(8,128)(2,1)S(1)}, u32[]{:S(2)}, u32[]{:S(2)}) async-start(bf16[16,32,512]{2,1,0:T(8,128)(2,1)} %broadcast_in_dim.7), calls=%async_computation.2 | async-start | bytes 1048576 | tf_op jit(solution)/shard_map/all_to_all | solution.py:188
  88.2 20.5 %collective-permute-start.8 = (bf16[128,1024]{1,0:T(8,128)(2,1)}, bf16[128,1024]{1,0:T(8,128)(2,1)}, u32[]{:S(2)}, u32[]{:S(2)}) collective-permute-start(bf16[128,1024]{1,0:T(8,128)(2,1)} %copy-done.8), channel_id=1, source_target_pairs={{0,2},{2,4},{4,6},{6,0},{1,3},{3,5},{5,7},{7,1},{8,10},{10,12},{12... | collective-permute-start | bytes 786440 | tf_op jit(solution)/shard_map/ppermute | solution.py:37
  91.3 17.4 %collective-permute-start.7 = (bf16[128,1024]{1,0:T(8,128)(2,1)}, bf16[128,1024]{1,0:T(8,128)(2,1)}, u32[]{:S(2)}, u32[]{:S(2)}) collective-permute-start(bf16[128,1024]{1,0:T(8,128)(2,1)} %copy-done.7), channel_id=1, source_target_pairs={{0,4},{2,6},{4,0},{6,2},{1,5},{3,7},{5,1},{7,3},{8,12},{10,14},{12... | collective-permute-start | bytes 786440 | tf_op jit(solution)/shard_map/ppermute | solution.py:37
  95.7 13.0 %collective-permute-start.6 = (bf16[128,1024]{1,0:T(8,128)(2,1)S(1)}, bf16[128,1024]{1,0:T(8,128)(2,1)}, u32[]{:S(2)}, u32[]{:S(2)}) collective-permute-start(bf16[128,1024]{1,0:T(8,128)(2,1)S(1)} %get-tuple-element.34), channel_id=1, source_target_pairs={{0,6},{2,0},{4,2},{6,4},{1,7},{3,1},{5,3},{7,5},{8,14},{10,8},{12,... | collective-permute-start | bytes 786440 | tf_op jit(solution)/shard_map/ppermute | solution.py:37
  104.9 5.8 %copy-start.1 = (bf16[1024,512]{1,0:T(8,128)(2,1)S(1)}, bf16[1024,512]{1,0:T(8,128)(2,1)}, u32[]{:S(2)}) copy-start(bf16[1024,512]{1,0:T(8,128)(2,1)} %base.1) | copy-start | bytes 3145732
  104.9 5.7 %collective-permute-start.5 = (bf16[512,512]{1,0:T(8,128)(2,1)S(1)}, bf16[512,512]{1,0:T(8,128)(2,1)S(1)}, u32[]{:S(2)}, u32[]{:S(2)}) collective-permute-start(bf16[512,512]{1,0:T(8,128)(2,1)S(1)} %bitcast.9), channel_id=1, source_target_pairs={{0,8},{8,0},{1,9},{9,1},{2,10},{10,2},{3,11},{11,3},{4,12},{12,4},... | collective-permute-start | bytes 1572872 | tf_op jit(solution)/shard_map/ppermute | solution.py:37

commit v4 on v3

--- a/solution.py
+++ b/solution.py
@@ -11,7 +11,8 @@
 outer_rate = 0.7
 momentum_coef = 0.9
 f32, bf16 = jnp.float32, jnp.bfloat16
-VMEM_LIMIT = 48 * 1024 * 1024
+LANES = 128
+MIB = 1024 * 1024
 
 SHAPE = (4, 3, 4, 2, 4, 2)
 NAMES = ("yh", "zh", "zl", "core", "x", "yl")
@@ -28,8 +29,8 @@
     return pl.BlockSpec(memory_space=pltpu.SMEM)
 
 
-def params():
-    return pltpu.CompilerParams(vmem_limit_bytes=VMEM_LIMIT)
+def params(mib=48):
+    return pltpu.CompilerParams(vmem_limit_bytes=mib * MIB)
 
 
 def shift(value, axis, by):
@@ -44,7 +45,8 @@
 def front_kernel(place, gain, exponents, tokens, values, *refs):
     (*blocks, keep, send), scratch = refs[: -len(FRONT)], refs[-len(FRONT) :]
     x, yl, core = place[0], place[1], place[2]
-    held, normed, delta, dequantized, token_in, block_out, delta_in, delta_out = scratch
+    held, normed, wide_gain, delta, dequantized = scratch[:5]
+    token_in, block_out, delta_in, delta_out = scratch[5:]
     peers, rows, block = normed.shape
     half = block // 2
 
@@ -56,6 +58,8 @@
         chunk(i).start()
     delta_copy = pltpu.make_async_copy(values, delta, delta_in)
     delta_copy.start()
+
+    wide_gain[...] = gain[...].astype(f32)
 
     total = jnp.zeros((rows, 128), f32)
     for i in range(peers):
@@ -69,9 +73,11 @@
     for k in (*range(1, peers), 0):
         first = lax.rem(x + k, peers) * block
         for at, part in ((0, yl), (half, 1 - yl)):
-            columns = pl.ds(pl.multiple_of(first + part * half, half), half)
-            piece = held[:, columns].astype(f32) * scale * gain[:, columns].astype(f32)
-            normed[k, :, at : at + half] = piece.astype(bf16)
+            for inner in range(0, half, LANES):
+                column = pl.multiple_of(first + part * half + inner, LANES)
+                piece = held[:, pl.ds(column, LANES)].astype(f32) * scale
+                piece = piece * wide_gain[pl.ds(column // LANES, 1), :]
+                normed[k, :, at + inner : at + inner + LANES] = piece.astype(bf16)
         outs.append(pltpu.make_async_copy(normed.at[k], blocks[k], block_out.at[k]))
         outs[-1].start()
 
@@ -93,7 +99,7 @@
         copy.wait()
 
 
-FRONT = ("held", "normed", "delta", "dequantized", "in", "out", "din", "dout")
+FRONT = ("held", "normed", "gain", "delta", "dequantized", "in", "out", "din", "dout")
 
 
 def front(place, tokens, gain, values, exponents):
@@ -111,6 +117,7 @@
         scratch_shapes=[
             pltpu.VMEM((rows, width), bf16),
             pltpu.VMEM((peers, rows, block), bf16),
+            pltpu.VMEM(gain.shape, f32),
             pltpu.VMEM((deep, across), bf16),
             pltpu.VMEM((2, deep // 2, across), bf16),
             dma((peers,)),
@@ -118,7 +125,7 @@
             dma,
             dma((2,)),
         ],
-        compiler_params=params(),
+        compiler_params=params(60),
         cost_estimate=pl.CostEstimate(
             flops=6 * rows * width + 4 * deep * across,
             bytes_accessed=4 * rows * width + 4 * deep * across,
@@ -285,7 +292,7 @@
     after = lax.optimization_barrier
 
     *blocks, keep, send = front(
-        place, tokens, norm_gain.reshape(1, -1), pseudo_grad[0], block_exponent[0].T
+        place, tokens, norm_gain.reshape(-1, LANES), pseudo_grad[0], block_exponent[0].T
     )
     arrived = [blocks[0]] + [shift(block, "x", k) for k, block in enumerate(blocks) if k]
     near = neighbour_weights(kv_weight)

time: 115 us -> 113 us (0.983)
  waiting for transfers between devices: 25.8 us -> 23.7 us
  other arithmetic: 5.07 us -> 6.81 us
  transfers between devices with their start and end apart: 12 -> 12, of which waited for: 3 -> 2; matrix products, arithmetic and copies ran while one was open for 4% -> 5% of each run, Pallas kernels for 5% -> 4%
where the time goes in v4:
time: 113 us; the launch traced here: 112 us
  starting transfers between devices  64 us (57%)
  waiting for transfers between devices  23.7 us (21%)
  Pallas kernels  12.3 us (11%)
  other arithmetic  6.81 us (6%)
  local copies, waits for them, and re-layouts  4.78 us (4%)
    ppermute x8, starting transfers between devices, shift(): return lax.ppermute(value, axis, [(i, (i + by) % n) for i in range(n)])  36.7 us
    all_to_all x1, waiting for transfers between devices, scatter_group(): parts = lax.all_to_all(parts, GROUP, 0, 0, tiled=True)  17.5 us
    all_to_all x1, starting transfers between devices, gather_group(): lax.all_to_all(jnp.broadcast_to(value, (group, *value.shape)), GROUP, 0,...  12.6 us
    all_to_all x1, starting transfers between devices, sum_thirds(): lax.all_to_all(jnp.broadcast_to(value, (third, *value.shape)), 'zh', 0, 0...  8.54 us
    all_to_all x1, waiting for transfers between devices, gather_group(): lax.all_to_all(jnp.broadcast_to(value, (group, *value.shape)), GROUP, 0,...  6.17 us
    pallas_call x1, Pallas kernels, project(): pl.pallas_call(project_kernel, out_shape=(jax.ShapeDtypeStruct((rows, wid...  4.8 us
    pallas_call x1, Pallas kernels, front(): pl.pallas_call(front_kernel, out_shape=(jax.ShapeDtypeStruct((rows, block...  4.47 us
    all_to_all x1, starting transfers between devices, scatter_group(): parts = lax.all_to_all(parts, GROUP, 0, 0, tiled=True)  4.24 us
  transfers between devices with their start and end apart: 12, of which 2 were waited for; matrix products, arithmetic and copies ran while one was open for 5% of the time, Pallas kernels for 4%

profile of v4, /device:TPU:1, one launch (start us, length us, event | category | flops | bytes accessed | tf_op | source)
XLA Modules:
  0.0 112.4 jit_solution(9132336162395103760)
XLA Ops:
  0.6 0.6 pad_add_fusion.place
  1.3 4.5 %front.1 = (bf16[128,2048]{1,0:T(8,128)(2,1)}, bf16[128,2048]{1,0:T(8,128)(2,1)}, bf16[128,2048]{1,0:T(8,128)(2,1)}, bf16[128,2048]{1,0:T(8,128)(2,1)}, bf16[512...) custom-call(s32[3]{0:T(128)} %pad_add_fusion.place, bf16[64,128]{1,0:T(8,128)(2,1)} %bitcast.13, s32[4,1024]{1,0:T(4,128)} %bitcast.14, ...), custom_call_target="tpu_custom_call" | custom-call | flops 8388608 | bytes 6291456 | tf_op jit(solution)/shard_map/front/pallas_call | solution.py:111
  5.8 0.0 copy-start.4
  5.8 12.6 %collective-permute-start = (bf16[512,512]{1,0:T(8,128)(2,1)}, bf16[512,512]{1,0:T(8,128)(2,1)S(1)}, u32[]{:S(2)}, u32[]{:S(2)}) collective-permute-start(bf16[512,512]{1,0:T(8,128)(2,1)} %get-tuple-element.21), channel_id=1, source_target_pairs={{0,8},{8,0},{1,9},{9,1},{2,10},{10,2},{3,11},{11,3},{4,12},{12,4},... | collective-permute-start | bytes 1572872 | tf_op jit(solution)/shard_map/ppermute | solution.py:38
  18.4 1.9 %collective-permute-start.4 = (bf16[2,1024,512]{2,1,0:T(8,128)(2,1)S(1)}, bf16[2,1024,512]{2,1,0:T(8,128)(2,1)}, u32[]{:S(2)}, u32[]{:S(2)}) collective-permute-start(bf16[2,1024,512]{2,1,0:T(8,128)(2,1)S(1)} %copy-done.3), channel_id=1, source_target_pairs={{0,1},{8,585},{1,192},{9,8},{192,193},{200,9},{193,384},{201,200},... | collective-permute-start | bytes 6291464 | tf_op jit(solution)/shard_map/ppermute | solution.py:286
  20.3 0.0 collective-permute-done
  20.3 2.0 %add_convert_fusion = bf16[512,512]{1,0:T(8,128)(2,1)} fusion(bf16[512,512]{1,0:T(8,128)(2,1)S(1)} %collective-permute-done, bf16[512,512]{1,0:T(8,128)(2,1)} %get-tuple-element.20), kind=kLoop, calls=%fused_computation.1 | loop fusion | flops 1048576 | bytes 1572864 | tf_op jit(solution)/shard_map/convert_element_type | solution.py:301
  22.3 4.2 %all-to-all-start = ((bf16[16,32,512]{2,1,0:T(8,128)(2,1)}), bf16[16,32,512]{2,1,0:T(8,128)(2,1)}, u32[]{:S(2)}, u32[]{:S(2)}) async-start(bf16[16,32,512]{2,1,0:T(8,128)(2,1)} %bitcast.7), calls=%async_computation | async-start | bytes 1048576 | tf_op jit(solution)/shard_map/all_to_all | solution.py:204
  26.5 2.4 %collective-permute-start.1 = (bf16[128,2048]{1,0:T(8,128)(2,1)}, bf16[128,2048]{1,0:T(8,128)(2,1)S(1)}, u32[]{:S(2)}, u32[]{:S(2)}) collective-permute-start(bf16[128,2048]{1,0:T(8,128)(2,1)} %get-tuple-element.23), channel_id=1, source_target_pairs={{0,2},{2,4},{4,6},{6,0},{1,3},{3,5},{5,7},{7,1},{8,10},{10,12},{12... | collective-permute-start | bytes 1572872 | tf_op jit(solution)/shard_map/ppermute | solution.py:38
  29.0 4.4 %collective-permute-start.2 = (bf16[128,2048]{1,0:T(8,128)(2,1)}, bf16[128,2048]{1,0:T(8,128)(2,1)}, u32[]{:S(2)}, u32[]{:S(2)}) collective-permute-start(bf16[128,2048]{1,0:T(8,128)(2,1)} %get-tuple-element.24), channel_id=1, source_target_pairs={{0,4},{2,6},{4,0},{6,2},{1,5},{3,7},{5,1},{7,3},{8,12},{10,14},{12... | collective-permute-start | bytes 1572872 | tf_op jit(solution)/shard_map/ppermute | solution.py:38
  33.3 3.1 %collective-permute-start.3 = (bf16[128,2048]{1,0:T(8,128)(2,1)}, bf16[128,2048]{1,0:T(8,128)(2,1)}, u32[]{:S(2)}, u32[]{:S(2)}) collective-permute-start(bf16[128,2048]{1,0:T(8,128)(2,1)} %get-tuple-element.25), channel_id=1, source_target_pairs={{0,6},{2,0},{4,2},{6,4},{1,7},{3,1},{5,3},{7,5},{8,14},{10,8},{12,... | collective-permute-start | bytes 1572872 | tf_op jit(solution)/shard_map/ppermute | solution.py:38
  36.4 17.5 %all-to-all-done = bf16[16,32,512]{2,1,0:T(8,128)(2,1)} async-done(((bf16[16,32,512]{2,1,0:T(8,128)(2,1)}), bf16[16,32,512]{2,1,0:T(8,128)(2,1)}, u32[]{:S(2)}, u32[]{:S(2)}) %all-to-all-start) | async-done | bytes 524320 | tf_op jit(solution)/shard_map/all_to_all | solution.py:204
  53.9 1.1 convert_reduce_fusion
  55.0 0.7 broadcast_in_dim.6
  55.7 8.5 %all-to-all-start.1 = ((f32[3,32,512]{2,1,0:T(8,128)}), f32[3,32,512]{2,1,0:T(8,128)}, u32[]{:S(2)}, u32[]{:S(2)}) async-start(f32[3,32,512]{2,1,0:T(8,128)} %broadcast_in_dim.6), calls=%async_computation.1 | async-start | bytes 393216 | tf_op jit(solution)/shard_map/all_to_all | solution.py:210
  64.2 0.0 collective-permute-done.1.refs_1_
  64.2 0.8 copy-done.5
  65.1 1.0 copy-done.6
  66.1 4.8 %project.1 = (f32[128,1024]{1,0:T(8,128)S(1)}, bf16[128,1024]{1,0:T(8,128)(2,1)S(1)}, bf16[128,1024]{1,0:T(8,128)(2,1)S(1)}, bf16[128,1024]{1,0:T(8,128)(2,1)S(1)}) custom-call(bf16[128,2048]{1,0:T(8,128)(2,1)S(1)} %copy-done.4, bf16[128,2048]{1,0:T(8,128)(2,1)S(1)} %copy-done.6, bf16[128,2048]{1,0:T(8,128)(2,1)} %collective-permute-done.2.refs_2_, ...), custom_call_target="tpu_custom_call" | custom-call | flops 2147483648 | bytes 8388608 | tf_op jit(solution)/shard_map/project/pallas_call | solution.py:253
  70.9 0.0 copy-start.7
  70.9 0.7 copy-done.7
  71.6 0.7 copy-done.8
  72.3 1.1 reduce_sum.19
  73.4 0.8 broadcast_in_dim.7
  74.3 12.6 %all-to-all-start.2 = ((bf16[16,32,512]{2,1,0:T(8,128)(2,1)}), bf16[16,32,512]{2,1,0:T(8,128)(2,1)S(1)}, u32[]{:S(2)}, u32[]{:S(2)}) async-start(bf16[16,32,512]{2,1,0:T(8,128)(2,1)} %broadcast_in_dim.7), calls=%async_computation.2 | async-start | bytes 1048576 | tf_op jit(solution)/shard_map/all_to_all | solution.py:195
  86.9 3.1 %collective-permute-start.8 = (bf16[128,1024]{1,0:T(8,128)(2,1)}, bf16[128,1024]{1,0:T(8,128)(2,1)}, u32[]{:S(2)}, u32[]{:S(2)}) collective-permute-start(bf16[128,1024]{1,0:T(8,128)(2,1)} %copy-done.8), channel_id=1, source_target_pairs={{0,2},{2,4},{4,6},{6,0},{1,3},{3,5},{5,7},{7,1},{8,10},{10,12},{12... | collective-permute-start | bytes 786440 | tf_op jit(solution)/shard_map/ppermute | solution.py:38
  90.0 4.4 %collective-permute-start.7 = (bf16[128,1024]{1,0:T(8,128)(2,1)}, bf16[128,1024]{1,0:T(8,128)(2,1)}, u32[]{:S(2)}, u32[]{:S(2)}) collective-permute-start(bf16[128,1024]{1,0:T(8,128)(2,1)} %copy-done.7), channel_id=1, source_target_pairs={{0,4},{2,6},{4,0},{6,2},{1,5},{3,7},{5,1},{7,3},{8,12},{10,14},{12... | collective-permute-start | bytes 786440 | tf_op jit(solution)/shard_map/ppermute | solution.py:38
  94.4 3.1 %collective-permute-start.6 = (bf16[128,1024]{1,0:T(8,128)(2,1)S(1)}, bf16[128,1024]{1,0:T(8,128)(2,1)}, u32[]{:S(2)}, u32[]{:S(2)}) collective-permute-start(bf16[128,1024]{1,0:T(8,128)(2,1)S(1)} %get-tuple-element.34), channel_id=1, source_target_pairs={{0,6},{2,0},{4,2},{6,4},{1,7},{3,1},{5,3},{7,5},{8,14},{10,8},{12,... | collective-permute-start | bytes 786440 | tf_op jit(solution)/shard_map/ppermute | solution.py:38
  97.4 6.2 %all-to-all-done.2 = bf16[16,32,512]{2,1,0:T(8,128)(2,1)S(1)} async-done(((bf16[16,32,512]{2,1,0:T(8,128)(2,1)}), bf16[16,32,512]{2,1,0:T(8,128)(2,1)S(1)}, u32[]{:S(2)}, u32[]{:S(2)}) %all-to-all-start.2) | async-done | bytes 524320 | tf_op jit(solution)/shard_map/all_to_all | solution.py:195
  103.6 3.7 %collective-permute-start.5 = (bf16[512,512]{1,0:T(8,128)(2,1)S(1)}, bf16[512,512]{1,0:T(8,128)(2,1)S(1)}, u32[]{:S(2)}, u32[]{:S(2)}) collective-permute-start(bf16[512,512]{1,0:T(8,128)(2,1)S(1)} %bitcast.10), channel_id=1, source_target_pairs={{0,8},{8,0},{1,9},{9,1},{2,10},{10,2},{3,11},{11,3},{4,12},{12,4},... | collective-permute-start | bytes 1572872 | tf_op jit(solution)/shard_map/ppermute | solution.py:38
  107.4 2.0 %add_convert_fusion.1 = bf16[128,1024]{1,0:T(8,128)(2,1)} fusion(bf16[128,1024]{1,0:T(8,128)(2,1)} %collective-permute-done.8, bf16[128,1024]{1,0:T(8,128)(2,1)} %collective-permute-done.7, f32[128,1024]{1,0:T(8,128)S(1)} %get-tuple-element.33, bf16[128,1024]{1,0:T(8,128)(2,1)} %collective-permute-done.6), kind=kLoop, calls=%fused_computation.2 | loop fusion | flops 917504 | bytes 1572864 | tf_op jit(solution)/shard_map/convert_element_type | solution.py:314
  109.4 3.0 %update.1 = (bf16[1024,512]{1,0:T(8,128)(2,1)}, f32[1024,512]{1,0:T(8,128)}) custom-call(s32[3]{0:T(128)S(1)} %copy-done.2, bf16[512,512]{1,0:T(8,128)(2,1)S(1)} %bitcast.11, bf16[512,512]{1,0:T(8,128)(2,1)S(1)} %collective-permute-done.5.other, bf16[1024,512]{1,0:T(8,128)(2,1)S(1)} %copy-done.1, f32[1024,512]{1,0:T(8,128)S(1)} %copy-done), custom_call_target="tpu_custom_call" | custom-call | flops 4194304 | bytes 7340032 | tf_op jit(solution)/shard_map/update/pallas_call | solution.py:168
  (21 shorter events, 0.1 us)
Async XLA Ops:
  0.6 17.7 %copy-start.3 = (bf16[2,1024,512]{2,1,0:T(8,128)(2,1)S(1)}, bf16[2,1024,512]{2,1,0:T(8,128)(2,1)}, u32[]{:S(2)}) copy-start(bf16[2,1024,512]{2,1,0:T(8,128)(2,1)} %refs_4_.1) | copy-start | bytes 6291460
  5.8 59.3 %copy-start.4 = (bf16[128,2048]{1,0:T(8,128)(2,1)S(1)}, bf16[128,2048]{1,0:T(8,128)(2,1)}, u32[]{:S(2)}) copy-start(bf16[128,2048]{1,0:T(8,128)(2,1)} %get-tuple-element.22.refs_0_) | copy-start | bytes 1572868
  5.8 14.5 %collective-permute-start = (bf16[512,512]{1,0:T(8,128)(2,1)}, bf16[512,512]{1,0:T(8,128)(2,1)S(1)}, u32[]{:S(2)}, u32[]{:S(2)}) collective-permute-start(bf16[512,512]{1,0:T(8,128)(2,1)} %get-tuple-element.21), channel_id=1, source_target_pairs={{0,8},{8,0},{1,9},{9,1},{2,10},{10,2},{3,11},{11,3},{4,12},{12,4},... | collective-permute-start | bytes 1572872 | tf_op jit(solution)/shard_map/ppermute | solution.py:38
  18.4 46.7 %collective-permute-start.4 = (bf16[2,1024,512]{2,1,0:T(8,128)(2,1)S(1)}, bf16[2,1024,512]{2,1,0:T(8,128)(2,1)}, u32[]{:S(2)}, u32[]{:S(2)}) collective-permute-start(bf16[2,1024,512]{2,1,0:T(8,128)(2,1)S(1)} %copy-done.3), channel_id=1, source_target_pairs={{0,1},{8,585},{1,192},{9,8},{192,193},{200,9},{193,384},{201,200},... | collective-permute-start | bytes 6291464 | tf_op jit(solution)/shard_map/ppermute | solution.py:286
  22.3 31.6 %all-to-all-start = ((bf16[16,32,512]{2,1,0:T(8,128)(2,1)}), bf16[16,32,512]{2,1,0:T(8,128)(2,1)}, u32[]{:S(2)}, u32[]{:S(2)}) async-start(bf16[16,32,512]{2,1,0:T(8,128)(2,1)} %bitcast.7), calls=%async_computation | async-start | bytes 1048576 | tf_op jit(solution)/shard_map/all_to_all | solution.py:204
  26.5 37.7 %collective-permute-start.1 = (bf16[128,2048]{1,0:T(8,128)(2,1)}, bf16[128,2048]{1,0:T(8,128)(2,1)S(1)}, u32[]{:S(2)}, u32[]{:S(2)}) collective-permute-start(bf16[128,2048]{1,0:T(8,128)(2,1)} %get-tuple-element.23), channel_id=1, source_target_pairs={{0,2},{2,4},{4,6},{6,0},{1,3},{3,5},{5,7},{7,1},{8,10},{10,12},{12... | collective-permute-start | bytes 1572872 | tf_op jit(solution)/shard_map/ppermute | solution.py:38
  29.0 36.1 %collective-permute-start.2 = (bf16[128,2048]{1,0:T(8,128)(2,1)}, bf16[128,2048]{1,0:T(8,128)(2,1)}, u32[]{:S(2)}, u32[]{:S(2)}) collective-permute-start(bf16[128,2048]{1,0:T(8,128)(2,1)} %get-tuple-element.24), channel_id=1, source_target_pairs={{0,4},{2,6},{4,0},{6,2},{1,5},{3,7},{5,1},{7,3},{8,12},{10,14},{12... | collective-permute-start | bytes 1572872 | tf_op jit(solution)/shard_map/ppermute | solution.py:38
  33.3 31.7 %collective-permute-start.3 = (bf16[128,2048]{1,0:T(8,128)(2,1)}, bf16[128,2048]{1,0:T(8,128)(2,1)}, u32[]{:S(2)}, u32[]{:S(2)}) collective-permute-start(bf16[128,2048]{1,0:T(8,128)(2,1)} %get-tuple-element.25), channel_id=1, source_target_pairs={{0,6},{2,0},{4,2},{6,4},{1,7},{3,1},{5,3},{7,5},{8,14},{10,8},{12,... | collective-permute-start | bytes 1572872 | tf_op jit(solution)/shard_map/ppermute | solution.py:38
  55.7 16.6 %all-to-all-start.1 = ((f32[3,32,512]{2,1,0:T(8,128)}), f32[3,32,512]{2,1,0:T(8,128)}, u32[]{:S(2)}, u32[]{:S(2)}) async-start(f32[3,32,512]{2,1,0:T(8,128)} %broadcast_in_dim.6), calls=%async_computation.1 | async-start | bytes 393216 | tf_op jit(solution)/shard_map/all_to_all | solution.py:210
  64.2 0.8 copy-start.5
  65.0 1.0 copy-start.6
  70.9 0.7 copy-start.7
  71.6 0.7 copy-start.8
  72.3 37.0 %copy-start = (f32[1024,512]{1,0:T(8,128)S(1)}, f32[1024,512]{1,0:T(8,128)}, u32[]{:S(2)}) copy-start(f32[1024,512]{1,0:T(8,128)} %momentum.1) | copy-start | bytes 6291460
  72.3 37.0 %copy-start.2 = (s32[3]{0:T(128)S(1)}, s32[3]{0:T(128)}, u32[]{:S(2)}) copy-start(s32[3]{0:T(128)} %pad_add_fusion.place) | copy-start | bytes 40
  74.3 29.3 %all-to-all-start.2 = ((bf16[16,32,512]{2,1,0:T(8,128)(2,1)}), bf16[16,32,512]{2,1,0:T(8,128)(2,1)S(1)}, u32[]{:S(2)}, u32[]{:S(2)}) async-start(bf16[16,32,512]{2,1,0:T(8,128)(2,1)} %broadcast_in_dim.7), calls=%async_computation.2 | async-start | bytes 1048576 | tf_op jit(solution)/shard_map/all_to_all | solution.py:195
  86.9 20.5 %collective-permute-start.8 = (bf16[128,1024]{1,0:T(8,128)(2,1)}, bf16[128,1024]{1,0:T(8,128)(2,1)}, u32[]{:S(2)}, u32[]{:S(2)}) collective-permute-start(bf16[128,1024]{1,0:T(8,128)(2,1)} %copy-done.8), channel_id=1, source_target_pairs={{0,2},{2,4},{4,6},{6,0},{1,3},{3,5},{5,7},{7,1},{8,10},{10,12},{12... | collective-permute-start | bytes 786440 | tf_op jit(solution)/shard_map/ppermute | solution.py:38
  90.0 17.4 %collective-permute-start.7 = (bf16[128,1024]{1,0:T(8,128)(2,1)}, bf16[128,1024]{1,0:T(8,128)(2,1)}, u32[]{:S(2)}, u32[]{:S(2)}) collective-permute-start(bf16[128,1024]{1,0:T(8,128)(2,1)} %copy-done.7), channel_id=1, source_target_pairs={{0,4},{2,6},{4,0},{6,2},{1,5},{3,7},{5,1},{7,3},{8,12},{10,14},{12... | collective-permute-start | bytes 786440 | tf_op jit(solution)/shard_map/ppermute | solution.py:38
  94.4 13.0 %collective-permute-start.6 = (bf16[128,1024]{1,0:T(8,128)(2,1)S(1)}, bf16[128,1024]{1,0:T(8,128)(2,1)}, u32[]{:S(2)}, u32[]{:S(2)}) collective-permute-start(bf16[128,1024]{1,0:T(8,128)(2,1)S(1)} %get-tuple-element.34), channel_id=1, source_target_pairs={{0,6},{2,0},{4,2},{6,4},{1,7},{3,1},{5,3},{7,5},{8,14},{10,8},{12,... | collective-permute-start | bytes 786440 | tf_op jit(solution)/shard_map/ppermute | solution.py:38
  103.6 5.8 %copy-start.1 = (bf16[1024,512]{1,0:T(8,128)(2,1)S(1)}, bf16[1024,512]{1,0:T(8,128)(2,1)}, u32[]{:S(2)}) copy-start(bf16[1024,512]{1,0:T(8,128)(2,1)} %base.1) | copy-start | bytes 3145732
  103.6 5.7 %collective-permute-start.5 = (bf16[512,512]{1,0:T(8,128)(2,1)S(1)}, bf16[512,512]{1,0:T(8,128)(2,1)S(1)}, u32[]{:S(2)}, u32[]{:S(2)}) collective-permute-start(bf16[512,512]{1,0:T(8,128)(2,1)S(1)} %bitcast.10), channel_id=1, source_target_pairs={{0,8},{8,0},{1,9},{9,1},{2,10},{10,2},{3,11},{11,3},{4,12},{12,4},... | collective-permute-start | bytes 1572872 | tf_op jit(solution)/shard_map/ppermute | solution.py:38
